TPU v7x, 32 devices: a whole 2x2x4 slice. The times are simulated.
32 devices in a mesh: wide: 8 (over y, x, core), narrow: 4 (over z).
Axes of the slice: x: 2, y: 2, z: 4, core: 2. Of those that a mesh axis runs over, the one named last changes fastest.
Arguments:
- sources: int32 [256, 256, 256], P('wide', 'narrow'), may hold values from 0 to 1
- labels: int32 [256, 256, 256], P('wide', 'narrow'), may hold values from 0 to 1, as said below
Outputs:
- distance: float32 [256, 256, 256], P('wide', 'narrow')
Inputs may be any that keep to these rules, and one draw needn't show every extreme that they name: labels marks the union of several periodic balls of radii between 16 and 42 cells; sources marks exactly the labelled cells that have an unlabelled neighbour along one of the six grid directions.
All inputs are finite; a program needn't handle non-finite values.
Results may differ from a plain program's by a relative error of at most 0.00022.
Values sent between devices are 32-bit elements; how exact they have to be, the bound alone decides.
A program may use at most 128 MiB of HBM per device.

v0:
```python
from functools import partial
import math

import jax
import jax.numpy as jnp
from jax import lax
from jax.sharding import PartitionSpec as P

highest = lax.Precision.HIGHEST


def extended(x, sides, width):
    for axis, dim in sides:
        peers, length = (lax.axis_size(axis), x.shape[dim])
        up = [(i, (i + 1) % peers) for i in range(peers)]
        down = [(j, i) for i, j in up]
        last = lax.slice_in_dim(x, length - width, length, axis=dim)
        initial = lax.slice_in_dim(x, 0, width, axis=dim)
        before = lax.ppermute(last, axis, up)
        after = lax.ppermute(initial, axis, down)
        x = jnp.concatenate([before, x, after], axis=dim)
    return x


def dft_tables(length):
    positions = jnp.arange(length, dtype=jnp.int32)
    phase_steps = positions[:, None] * positions[None, :] % length
    angles = phase_steps.astype(jnp.float32) * (2.0 * math.pi / length)
    return (jnp.cos(angles), jnp.sin(angles))


def rotate(pattern, complex_pair, cosine, sine_table, direction_sign):
    contract = partial(jnp.einsum, pattern, precision=highest)
    real_part = complex_pair[0]
    imag_part = complex_pair[1]
    new_real = contract(real_part, cosine) - direction_sign * contract(imag_part, sine_table)
    new_imag = contract(imag_part, cosine) + direction_sign * contract(real_part, sine_table)
    return jnp.stack((new_real, new_imag))


def turn_narrow(stacked):
    return lax.all_to_all(stacked, "narrow", split_axis=2, concat_axis=3, tiled=True)


def turn_wide(stacked):
    return lax.all_to_all(stacked, "wide", split_axis=2, concat_axis=3, tiled=True)


def forward(real_fields, tables):
    cosine, sine_table = tables
    fields = real_fields.shape[0]
    length = real_fields.shape[3]
    wide_size = lax.axis_size("wide")
    narrow_size = lax.axis_size("narrow")
    span_wide = length // wide_size
    span_narrow = length // narrow_size
    along_z = jnp.stack(
        (
            jnp.einsum("fxyz,zk->fkxy", real_fields, cosine, precision=highest),
            -jnp.einsum("fxyz,zk->fkxy", real_fields, sine_table, precision=highest),
        )
    )
    arrived = turn_narrow(along_z.reshape(2, fields, length, span_wide * span_narrow))
    arrived = arrived.reshape(2, fields, span_narrow, narrow_size, span_wide, span_narrow)
    along_y = rotate(
        "fknxj,njl->flkx",
        arrived,
        cosine.reshape(narrow_size, span_narrow, length),
        sine_table.reshape(narrow_size, span_narrow, length),
        -1.0,
    )
    arrived = turn_wide(along_y.reshape(2, fields, length, span_narrow * span_wide))
    arrived = arrived.reshape(2, fields, span_wide, wide_size, span_narrow, span_wide)
    return rotate(
        "flwki,wim->flkm",
        arrived,
        cosine.reshape(wide_size, span_wide, length),
        sine_table.reshape(wide_size, span_wide, length),
        -1.0,
    )


def inverse(spectra, tables):
    cosine, sine_table = tables
    fields = spectra.shape[1]
    length = spectra.shape[4]
    wide_size = lax.axis_size("wide")
    narrow_size = lax.axis_size("narrow")
    span_wide = length // wide_size
    span_narrow = length // narrow_size
    along_x = rotate("flkm,mx->fxlk", spectra, cosine, sine_table, 1.0)
    arrived = turn_wide(along_x.reshape(2, fields, length, span_wide * span_narrow))
    arrived = arrived.reshape(2, fields, span_wide, wide_size, span_wide, span_narrow)
    along_y = rotate(
        "fxwlk,wly->fyxk",
        arrived,
        cosine.reshape(wide_size, span_wide, length),
        sine_table.reshape(wide_size, span_wide, length),
        1.0,
    )
    arrived = turn_narrow(along_y.reshape(2, fields, length, span_wide * span_narrow))
    arrived = arrived.reshape(2, fields, span_narrow, narrow_size, span_wide, span_narrow)
    real_values = jnp.einsum(
        "fynxk,nkz->fxyz",
        arrived[0],
        cosine.reshape(narrow_size, span_narrow, length),
        precision=highest,
    ) - jnp.einsum(
        "fynxk,nkz->fxyz",
        arrived[1],
        sine_table.reshape(narrow_size, span_narrow, length),
        precision=highest,
    )
    return real_values / float(length) ** 3


def eigen_sine(wavenumber, length):
    angles = wavenumber.astype(jnp.float32) * (2.0 * math.pi / length)
    return (2.0 - 2.0 * jnp.cos(angles), jnp.sin(angles))


def central_last(values):
    return 0.5 * (jnp.roll(values, -1, values.ndim - 1) - jnp.roll(values, 1, values.ndim - 1))


def normalize(gradients, grad_floor):
    magnitude = jnp.sqrt(jnp.sum(gradients * gradients, axis=0))
    return -gradients / jnp.maximum(magnitude, grad_floor)


def per_device(sources, labels):
    length = sources.shape[2]
    heat_time = (length / 8.0) ** 2
    grad_floor = 0.04 / heat_time
    tables = dft_tables(length)
    span_wide = length // lax.axis_size("wide")
    span_narrow = length // lax.axis_size("narrow")
    wave_wide = lax.axis_index("wide") * span_wide + jnp.arange(span_wide, dtype=jnp.int32)
    wave_narrow = lax.axis_index("narrow") * span_narrow + jnp.arange(span_narrow, dtype=jnp.int32)
    wave_full = jnp.arange(length, dtype=jnp.int32)
    eigen_wide, sine_wide = eigen_sine(wave_wide, length)
    eigen_narrow, sine_narrow = eigen_sine(wave_narrow, length)
    eigen_full, sine_full = eigen_sine(wave_full, length)
    laplace = eigen_wide[:, None, None] + eigen_narrow[None, :, None] + eigen_full[None, None, :]
    anchor = (
        (wave_wide[:, None, None] == 0)
        & (wave_narrow[None, :, None] == 0)
        & (wave_full[None, None, :] == 0)
    )
    source = sources.astype(jnp.float32)
    spectrum = forward(source[None], tables)
    heat_hat = spectrum / (1.0 + heat_time * laplace)
    heat_field = inverse(heat_hat, tables)[0]
    padded = extended(heat_field, (("wide", 0), ("narrow", 1)), 1)
    gradients = jnp.stack(
        (
            0.5 * (padded[2:, 1:-1] - padded[:-2, 1:-1]),
            0.5 * (padded[1:-1, 2:] - padded[1:-1, :-2]),
            central_last(heat_field),
        )
    )
    flow = normalize(gradients, grad_floor)
    rims = extended(flow[:2], (("wide", 1), ("narrow", 2)), 1)
    divergence = (
        0.5 * (rims[0, 2:, 1:-1] - rims[0, :-2, 1:-1])
        + 0.5 * (rims[1, 1:-1, 2:] - rims[1, 1:-1, :-2])
        + central_last(flow[2])
    )
    div_hat = forward(divergence[None], tables)[:, 0]
    laplace_safe = jnp.where(anchor, 1.0, laplace)
    potential_hat = jnp.where(anchor[None], 0.0, -div_hat / laplace_safe[None])
    potential = inverse(potential_hat[:, None], tables)[0]
    signs = (2 * labels - 1).astype(jnp.float32)
    return signs * potential


def solution(mesh):
    return jax.shard_map(
        per_device,
        mesh=mesh,
        in_specs=(P("wide", "narrow", None), P("wide", "narrow", None)),
        out_specs=P("wide", "narrow", None),
        check_vma=False,
    )
```

profile of v0, /device:TPU:0, one launch (start us, length us, event | category | flops | bytes accessed | tf_op | source)
XLA Modules:
  0.0 1196.6 jit_solution(16768166214655969382)
XLA Ops:
  18.3 8.0 pad_maximum_fusion.1
  32.8 93.4 %all-to-all-done = f32[2,1,256,2048]{3,0,1,2:T(2,128)} async-done(((f32[2,1,256,2048]{3,0,1,2:T(2,128)}), f32[2,1,256,2048]{3,0,1,2:T(2,128)}, u32[]{:S(2)}, u32[]{:S(2)}) %all-to-all-start) | async-done | bytes 4194336 | tf_op jit(solution)/shard_map/all_to_all | solution.py:42
  135.6 10.6 fusion.21
  157.9 10.2 fusion.55
  180.9 11.0 copy.115
  198.7 47.1 %all-to-all-done.1 = f32[2,1,256,2048]{3,1,0,2:T(1,128)} async-done(((f32[2,1,256,2048]{3,1,0,2:T(1,128)}), f32[2,1,256,2048]{3,1,0,2:T(1,128)}, u32[]{:S(2)}, u32[]{:S(2)}) %all-to-all-start.1) | async-done | bytes 4194336 | tf_op jit(solution)/shard_map/all_to_all | solution.py:46
  271.3 9.2 fusion.121
  295.8 8.0 fusion.51
  338.0 51.6 %all_to_all.120 = f32[2,1,256,2048]{3,0,1,2:T(2,128)S(1)} all-to-all(f32[2,1,256,2048]{3,0,1,2:T(2,128)S(1)} %pad_maximum_fusion.3), channel_id=1, replica_groups=mesh['wide'=8,'narrow'=4] {'wide'}, dimensions={2} | all-to-all | bytes 8388608 | tf_op jit(solution)/shard_map/all_to_all | solution.py:46
  398.2 11.2 fusion.117
  414.2 11.2 fusion.115
  425.4 9.3 bitcast_subtract_fusion.3
  439.5 11.8 bitcast_add_fusion.1
  462.7 95.5 %all_to_all.121 = f32[2,1,256,2048]{3,0,1,2:T(2,128)S(1)} all-to-all(f32[2,1,256,2048]{3,0,1,2:T(2,128)S(1)} %pad_maximum_fusion.4), channel_id=1, replica_groups=mesh['wide'=8,'narrow'=4] {'narrow'}, dimensions={2} | all-to-all | bytes 8388608 | tf_op jit(solution)/shard_map/all_to_all | solution.py:42
  565.4 9.5 fusion.7
  579.8 10.2 fusion.49
  640.0 94.9 %all_to_all.122 = f32[2,1,256,2048]{3,1,0,2:T(1,128)S(1)} all-to-all(f32[2,1,256,2048]{3,1,0,2:T(1,128)} %copy.138), channel_id=1, replica_groups=mesh['wide'=8,'narrow'=4] {'narrow'}, dimensions={2} | all-to-all | bytes 8388608 | tf_op jit(solution)/shard_map/all_to_all | solution.py:42
  742.0 10.8 fusion.13
  764.5 10.0 fusion.46
  787.2 11.0 copy.146
  804.8 48.7 %all-to-all-done.5 = f32[2,1,256,2048]{3,1,0,2:T(1,128)} async-done(((f32[2,1,256,2048]{3,1,0,2:T(1,128)}), f32[2,1,256,2048]{3,1,0,2:T(1,128)}, u32[]{:S(2)}, u32[]{:S(2)}) %all-to-all-start.5) | async-done | bytes 4194336 | tf_op jit(solution)/shard_map/all_to_all | solution.py:46
  865.9 10.4 fusion.113
  882.3 9.2 fusion.111
  891.6 9.7 fusion.44
  943.8 51.6 %all_to_all.123 = f32[2,1,256,2048]{3,0,1,2:T(2,128)S(1)} all-to-all(f32[2,1,256,2048]{3,0,1,2:T(2,128)S(1)} %pad_maximum_fusion.7), channel_id=1, replica_groups=mesh['wide'=8,'narrow'=4] {'wide'}, dimensions={2} | all-to-all | bytes 8388608 | tf_op jit(solution)/shard_map/all_to_all | solution.py:46
  1004.0 11.2 fusion.109
  1019.7 11.2 fusion.107
  1031.0 9.5 bitcast_subtract_fusion.1
  1045.3 11.8 bitcast_add_fusion
  1068.5 95.5 %all_to_all.124 = f32[2,1,256,2048]{3,0,1,2:T(2,128)S(1)} all-to-all(f32[2,1,256,2048]{3,0,1,2:T(2,128)S(1)} %pad_maximum_fusion.8), channel_id=1, replica_groups=mesh['wide'=8,'narrow'=4] {'narrow'}, dimensions={2} | all-to-all | bytes 8388608 | tf_op jit(solution)/shard_map/all_to_all | solution.py:42
  1171.2 9.5 fusion.3
  1185.6 10.8 bitcast_multiply_fusion
  (181 shorter events, 371.9 us)
Async XLA Ops:
  0.0 5.9 copy-start.9
  26.3 99.9 %all-to-all-start = ((f32[2,1,256,2048]{3,0,1,2:T(2,128)}), f32[2,1,256,2048]{3,0,1,2:T(2,128)}, u32[]{:S(2)}, u32[]{:S(2)}) async-start(f32[2,1,256,2048]{3,0,1,2:T(2,128)} %pad_maximum_fusion.1), calls=%async_computation | async-start | bytes 8388608 | tf_op jit(solution)/shard_map/all_to_all | solution.py:42
  135.6 10.6 copy-start
  191.9 53.9 %all-to-all-start.1 = ((f32[2,1,256,2048]{3,1,0,2:T(1,128)}), f32[2,1,256,2048]{3,1,0,2:T(1,128)}, u32[]{:S(2)}, u32[]{:S(2)}) async-start(f32[2,1,256,2048]{3,1,0,2:T(1,128)} %copy.115), calls=%async_computation.1 | async-start | bytes 8388608 | tf_op jit(solution)/shard_map/all_to_all | solution.py:46
  271.3 9.2 copy-start.2
  280.6 15.2 %slice-start = ((s8[8388608]{0:T(1024)(128)(4,1)}), s8[4194304]{0:T(1024)(128)(4,1)S(1)}, s32[]{:S(2)}) async-start(s8[8388608]{0:T(1024)(128)(4,1)} %bitcast.398), calls=%async_computation.8 | async-start | bytes 8388608
  288.2 7.6 slice-start.1
  304.5 5.7 copy-start.4
  326.4 6.3 copy-start.15
  398.2 11.2 copy-start.12
  414.1 11.3 copy-start.7
  414.1 11.3 copy-start.18
  590.1 2.0 collective-permute-start
  590.1 4.6 collective-permute-start.1
  594.8 4.0 collective-permute-start.2
  596.3 5.7 collective-permute-start.3
  606.2 3.9 collective-permute-start.4
  606.3 5.3 collective-permute-start.5
  611.7 4.5 collective-permute-start.6
  611.8 6.2 collective-permute-start.7
  742.0 10.8 copy-start.1
  798.3 55.2 %all-to-all-start.5 = ((f32[2,1,256,2048]{3,1,0,2:T(1,128)}), f32[2,1,256,2048]{3,1,0,2:T(1,128)}, u32[]{:S(2)}, u32[]{:S(2)}) async-start(f32[2,1,256,2048]{3,1,0,2:T(1,128)} %copy.146), calls=%async_computation.5 | async-start | bytes 8388608 | tf_op jit(solution)/shard_map/all_to_all | solution.py:46
  865.9 10.4 copy-start.13
  882.3 9.2 copy-start.10
  882.3 19.0 %slice-start.2 = ((s8[8388608]{0:T(1024)(128)(4,1)}), s8[4194304]{0:T(1024)(128)(4,1)S(1)}, s32[]{:S(2)}) async-start(s8[8388608]{0:T(1024)(128)(4,1)} %bitcast.400), calls=%async_computation.10 | async-start | bytes 8388608
  891.6 9.7 slice-start.3
  901.3 7.6 copy-start.11
  910.0 5.7 copy-start.3
  932.2 6.3 copy-start.16
  1004.0 11.3 copy-start.14
  1019.7 11.3 copy-start.8
  1019.7 11.3 copy-start.19
  (3 other events, 8.7 us)
where the time goes:
time: 1210 us; the launch traced here: 1200 us
  blocking collectives  389 us (32%)
  matrix products  314 us (26%)
  local copies, waits for them, and re-layouts  218 us (18%)
  waiting for transfers between devices  204 us (17%)
  other arithmetic  47.4 us (4%)
  starting transfers between devices  22.5 us (2%)
    all_to_all x3, blocking collectives, turn_narrow(): lax.all_to_all(stacked, 'narrow', split_axis=2, concat_axis=3, tiled=True)  286 us
    all_to_all x2, blocking collectives, turn_wide(): lax.all_to_all(stacked, 'wide', split_axis=2, concat_axis=3, tiled=True)  103 us
    all_to_all x2, waiting for transfers between devices, turn_wide(): lax.all_to_all(stacked, 'wide', split_axis=2, concat_axis=3, tiled=True)  95.8 us
    all_to_all x1, waiting for transfers between devices, turn_narrow(): lax.all_to_all(stacked, 'narrow', split_axis=2, concat_axis=3, tiled=True)  93.4 us
    another operation x10, local copies, waits for them, and re-layouts, rotate(): return jnp.stack((new_real, new_imag))  68.9 us
    dot_general x8, matrix products, rotate(): contract(real_part, cosine)  68.1 us
    another operation x16, local copies, waits for them, and re-layouts  67.1 us
    dot_general x8, matrix products, rotate(): contract(imag_part, sine_table)  66 us
  transfers between devices with their start and end apart: 11, of which 11 were waited for; matrix products, arithmetic and copies ran while one was open for 1% of the time, Pallas kernels for 0%

commit v1 on v0

v1 whole, which is shorter than its diff:
```python
from functools import partial
import math

import jax
import jax.numpy as jnp
from jax import lax
from jax.experimental import pallas as pl
from jax.experimental.pallas import tpu as pltpu
from jax.sharding import PartitionSpec as P
import numpy as np

highest = lax.Precision.HIGHEST
moment_rows = 8


def cas_table(length):
    positions = np.arange(length)
    angles = (positions[:, None] * positions[None, :] % length) * (2.0 * math.pi / length)
    return (np.cos(angles) + np.sin(angles)).astype(np.float32)


def decay_table(length, shift):
    eigen = 4.0 * np.sin(np.pi * np.arange(length) / length) ** 2
    lam = shift + eigen[:, None] + eigen[None, :]
    return np.where(lam > 0.0, np.exp(-2.0 * np.arcsinh(0.5 * np.sqrt(lam))), 0.0).astype(np.float32)


def column_tables(length, blocks):
    span = length // blocks
    const = (length * length - 1.0) / (12.0 * length)
    j = np.arange(span, dtype=np.float64)
    gap = np.abs(j[:, None] - j[None, :])
    parts = [gap * (gap - length) / (2.0 * length) + const]
    centred = j - (span - 1) / 2.0
    for delta in range(1, blocks):
        a = centred + length - span * delta
        rows = np.zeros((span, moment_rows))
        rows[:, 0] = (a * a - length * a) / (2.0 * length) + const
        rows[:, 1] = -(2.0 * a - length) / (2.0 * length)
        rows[:, 2] = 1.0 / (2.0 * length)
        parts.append(rows)
    moments = np.zeros((moment_rows, span))
    moments[0], moments[1], moments[2] = 1.0, centred, centred * centred
    return np.concatenate(parts, axis=1).astype(np.float32), moments.astype(np.float32)


def power(base, exponent):
    result = None
    while exponent:
        if exponent & 1:
            result = base if result is None else result * base
        base = base * base
        exponent >>= 1
    return result


def solve_kernel(n, field, table, decay, scale, green, moments, mask, out, work, sent, arrived, send_sem, recv_sem):
    span, layers, length = work.shape
    lanes = 128
    group = lanes // layers
    chunks = span // group
    me = lax.axis_index("narrow")
    barrier = pltpu.get_barrier_semaphore()
    for step in range(1, n):
        pl.semaphore_signal(
            barrier, inc=1, device_id={"narrow": lax.rem(me + step, n)}, device_id_type=pl.DeviceIdType.MESH
        )

    def to_waves(c, carry):
        columns = pl.ds(pl.multiple_of(c * lanes, lanes), lanes)
        block = lax.dot_general(
            field[:, columns].T, table[...], (((1,), (0,)), ((), ())), precision=highest,
            preferred_element_type=jnp.float32,
        )
        work[pl.ds(c * group, group)] = block.reshape(group, layers, length)
        return carry

    lax.fori_loop(0, chunks, to_waves, 0)
    r = decay[...]
    s = scale[...]
    column = work[:, 0, :]
    sent[2 * layers :, :] = jnp.dot(moments[...], column, precision=highest, preferred_element_type=jnp.float32)

    def ahead(j, v):
        v = work[j] + r * v
        work[j] = v
        return v

    v_last = lax.fori_loop(0, span, ahead, jnp.zeros_like(r), unroll=4)

    def back(i, u):
        j = span - 1 - i
        u = s * work[j] + r * u
        work[j] = u
        return u

    u_first = lax.fori_loop(0, span, back, jnp.zeros_like(r), unroll=4)
    sent[0:layers, :] = v_last
    sent[layers : 2 * layers, :] = u_first
    pl.semaphore_wait(barrier, n - 1)
    copies = []
    for step in range(1, n):
        copy = pltpu.make_async_remote_copy(
            src_ref=sent,
            dst_ref=arrived.at[n - 1 - step],
            send_sem=send_sem.at[step - 1],
            recv_sem=recv_sem.at[n - 1 - step],
            device_id={"narrow": lax.rem(me + step, n)},
            device_id_type=pl.DeviceIdType.MESH,
        )
        copy.start()
        copies.append(copy)
    for copy in copies:
        copy.wait()
    stacked = jnp.concatenate([column] + [arrived[d, 2 * layers :, :] for d in range(n - 1)], axis=0)
    extra = jnp.dot(green[...], stacked, precision=highest, preferred_element_type=jnp.float32) * mask[...]
    last = [v_last] + [arrived[d, 0:layers, :] for d in range(n - 1)]
    first = [u_first] + [arrived[d, layers : 2 * layers, :] for d in range(n - 1)]
    q = power(r, span)
    close = 1.0 / (1.0 - power(q, n))
    factor = s / (1.0 - r * r)
    tail = q * r
    edge = r - tail * q
    alphas = []
    for t in range(n):
        total = last[t % n]
        for k in range(n - 2, -1, -1):
            total = last[(t - 1 - k) % n] + q * total
        alphas.append(total * close * factor)
    begin = [first[t] + alphas[t] * edge for t in range(n)]
    total = begin[0]
    for k in range(n - 2, -1, -1):
        total = begin[(1 + k) % n] + q * total
    inflow = total * close

    def add_ahead(j, p):
        work[j] = work[j] + p
        return p * r

    lax.fori_loop(0, span, add_ahead, alphas[0] * r, unroll=4)

    def add_back(i, p):
        j = span - 1 - i
        work[j] = work[j] + p
        return p * r

    lax.fori_loop(0, span, add_back, (inflow - alphas[0] * tail) * r, unroll=4)
    work[:, 0, :] = work[:, 0, :] + extra

    def from_waves(c, carry):
        columns = pl.ds(pl.multiple_of(c * lanes, lanes), lanes)
        block = work[pl.ds(c * group, group)].reshape(lanes, length)
        out[:, columns] = lax.dot_general(
            table[...], block, (((1,), (1,)), ((), ())), precision=highest, preferred_element_type=jnp.float32
        )
        return carry

    lax.fori_loop(0, chunks, from_waves, 0)


def solve_lines(field, tables, decay, scale, mask, layers):
    length, columns = field.shape
    n = lax.axis_size("narrow")
    span = columns // layers
    rows = 2 * layers + moment_rows
    vmem = pl.BlockSpec(memory_space=pltpu.VMEM)
    return pl.pallas_call(
        partial(solve_kernel, n),
        out_shape=jax.ShapeDtypeStruct((length, columns), jnp.float32),
        in_specs=[vmem] * 7,
        out_specs=vmem,
        scratch_shapes=[
            pltpu.VMEM((span, layers, length), jnp.float32),
            pltpu.VMEM((rows, length), jnp.float32),
            pltpu.VMEM((n - 1, rows, length), jnp.float32),
            pltpu.SemaphoreType.DMA((n - 1,)),
            pltpu.SemaphoreType.DMA((n - 1,)),
        ],
        compiler_params=pltpu.CompilerParams(
            collective_id=0, has_side_effects=True, vmem_limit_bytes=40 * 1024 * 1024
        ),
        cost_estimate=pl.CostEstimate(
            flops=4 * length * length * columns, bytes_accessed=8 * length * columns, transcendentals=0
        ),
        name="lines",
    )(field, tables[0], decay, scale, tables[1], tables[2], mask)


def solve(real_field, tables, decay, scale, mask):
    table = tables[0]
    span_wide, span_narrow, length = real_field.shape
    wide = lax.axis_size("wide")
    layers = length // wide
    waves = jnp.einsum("xyz,zk->xyk", real_field, table, precision=highest)
    blocks = waves.reshape(span_wide, span_narrow, wide, layers).transpose(2, 0, 1, 3)
    arrived = lax.all_to_all(
        blocks.reshape(wide, span_wide, span_narrow * layers), "wide", split_axis=0, concat_axis=0, tiled=True
    )
    lines = solve_lines(arrived.reshape(length, span_narrow * layers), tables, decay, scale, mask, layers)
    returned = lax.all_to_all(
        lines.reshape(wide, span_wide, span_narrow * layers), "wide", split_axis=0, concat_axis=0, tiled=True
    )
    waves = returned.reshape(wide, span_wide, span_narrow, layers).transpose(1, 2, 0, 3)
    return jnp.einsum("xyk,kz->xyz", waves.reshape(span_wide, span_narrow, length), table, precision=highest)


def extended(x, sides, width):
    for axis, dim in sides:
        peers, length = (lax.axis_size(axis), x.shape[dim])
        up = [(i, (i + 1) % peers) for i in range(peers)]
        down = [(j, i) for i, j in up]
        last = lax.slice_in_dim(x, length - width, length, axis=dim)
        initial = lax.slice_in_dim(x, 0, width, axis=dim)
        before = lax.ppermute(last, axis, up)
        after = lax.ppermute(initial, axis, down)
        x = jnp.concatenate([before, x, after], axis=dim)
    return x


def central_last(values):
    return 0.5 * (jnp.roll(values, -1, values.ndim - 1) - jnp.roll(values, 1, values.ndim - 1))


def flow_divergence(heat_field, grad_floor):
    padded = extended(heat_field, (("wide", 0), ("narrow", 1)), 2)
    grad_x = 0.5 * (padded[2:, 1:-1] - padded[:-2, 1:-1])
    grad_y = 0.5 * (padded[1:-1, 2:] - padded[1:-1, :-2])
    grad_z = central_last(padded[1:-1, 1:-1])
    magnitude = jnp.sqrt(grad_x * grad_x + grad_y * grad_y + grad_z * grad_z)
    inverse = -1.0 / jnp.maximum(magnitude, grad_floor)
    flow_x = grad_x * inverse
    flow_y = grad_y * inverse
    flow_z = (grad_z * inverse)[1:-1, 1:-1]
    return (
        0.5 * (flow_x[2:, 1:-1] - flow_x[:-2, 1:-1])
        + 0.5 * (flow_y[1:-1, 2:] - flow_y[1:-1, :-2])
        + central_last(flow_z)
    )


def per_device(sources, labels):
    length = sources.shape[2]
    heat_time = (length / 8.0) ** 2
    grad_floor = 0.04 / heat_time
    wide = lax.axis_size("wide")
    layers = length // wide
    place = lax.axis_index("wide")
    green, moments = column_tables(length, lax.axis_size("narrow"))
    tables = (jnp.asarray(cas_table(length)), jnp.asarray(green), jnp.asarray(moments))

    def mine(table):
        return lax.dynamic_slice_in_dim(jnp.asarray(table), place * layers, layers, axis=0)

    heat_decay = mine(decay_table(length, 1.0 / heat_time))
    line_decay = mine(decay_table(length, 0.0))
    corner = (jnp.arange(length, dtype=jnp.int32)[None, :] == 0) & (place == 0)
    norm = float(length) ** 2
    heat_field = solve(
        sources.astype(jnp.float32), tables, heat_decay, heat_decay * (1.0 / (heat_time * norm)),
        jnp.zeros((1, length), jnp.float32),
    )
    divergence = flow_divergence(heat_field, grad_floor)
    potential = solve(
        divergence, tables, line_decay, line_decay * (-1.0 / norm), jnp.where(corner, -1.0 / norm, 0.0)
    )
    signs = (2 * labels - 1).astype(jnp.float32)
    return signs * potential


def solution(mesh):
    return jax.shard_map(
        per_device,
        mesh=mesh,
        in_specs=(P("wide", "narrow", None), P("wide", "narrow", None)),
        out_specs=P("wide", "narrow", None),
        check_vma=False,
    )
```

time: 1210 us -> 268 us (0.22); the launches traced: 1200 us -> 267 us
  blocking collectives: 389 us -> 60.1 us
  matrix products: 314 us -> 29.4 us
  local copies, waits for them, and re-layouts: 218 us -> 57.7 us
  waiting for transfers between devices: 204 us -> 58.6 us
  other arithmetic: 47.4 us -> 8.33 us
  Pallas kernels: 0 us -> 37.7 us
    all_to_all x5 -> x2, blocking collectives: 389 us -> 60.1 us  [solve(): lax.all_to_all(lines.reshape(wide, span_wide, span_narrow * layers), 'wid...]
    dot_general x40 -> x4, matrix products: 314 us -> 29.4 us  [the longest x2 19.2 us: solve(): jnp.einsum('xyk,kz->xyz', waves.reshape(span_wide, span_narrow, length),...]
    another operation x30 -> x0, local copies, waits for them, and re-layouts: 155 us -> none  [the longest x10 68.9 us: rotate(): return jnp.stack((new_real, new_imag))]
    all_to_all x3 -> x2, waiting for transfers between devices: 189 us -> 51.7 us  [solve(): lax.all_to_all(blocks.reshape(wide, span_wide, span_narrow * layers), 'wi...]
    pallas_call x0 -> x2, Pallas kernels: none -> 37.7 us  [solve_lines(): pl.pallas_call(partial(solve_kernel, n), out_shape=jax.ShapeDtypeStruct((...]
    another operation x9 -> x0, other arithmetic: 35.6 us -> none  [the longest x6 26 us: rotate(): return jnp.stack((new_real, new_imag))]
    transpose x0 -> x4, local copies, waits for them, and re-layouts: none -> 27.8 us  [the longest x2 13.9 us: solve(): waves.reshape(span_wide, span_narrow, wide, layers).transpose(2, 0, 1, 3)]
    all_to_all x8 -> x0, local copies, waits for them, and re-layouts: 26 us -> none  [the longest x4 14.1 us: turn_wide(): lax.all_to_all(stacked, 'wide', split_axis=2, concat_axis=3, tiled=True)]
  transfers between devices with their start and end apart: 11 -> 6, of which waited for: 11 -> 5; matrix products, arithmetic and copies ran while one was open for 1% -> 1% of each run, Pallas kernels for 0% -> 0%
where the time goes in v1:
time: 268 us; the launch traced here: 267 us
  blocking collectives  60.1 us (22%)
  waiting for transfers between devices  58.6 us (22%)
  local copies, waits for them, and re-layouts  57.7 us (22%)
  Pallas kernels  37.7 us (14%)
  matrix products  29.4 us (11%)
  starting transfers between devices  15.5 us (6%)
  other arithmetic  8.33 us (3%)
    all_to_all x2, blocking collectives, solve(): lax.all_to_all(lines.reshape(wide, span_wide, span_narrow * layers), 'wid...  60.1 us
    all_to_all x2, waiting for transfers between devices, solve(): lax.all_to_all(blocks.reshape(wide, span_wide, span_narrow * layers), 'wi...  51.7 us
    pallas_call x2, Pallas kernels, solve_lines(): pl.pallas_call(partial(solve_kernel, n), out_shape=jax.ShapeDtypeStruct((...  37.7 us
    dot_general x2, matrix products, solve(): jnp.einsum('xyk,kz->xyz', waves.reshape(span_wide, span_narrow, length),...  19.2 us
    reshape x2, local copies, waits for them, and re-layouts, solve(): blocks.reshape(wide, span_wide, span_narrow * layers)  15 us
    transpose x2, local copies, waits for them, and re-layouts, solve(): waves.reshape(span_wide, span_narrow, wide, layers).transpose(2, 0, 1, 3)  13.9 us
    transpose x2, local copies, waits for them, and re-layouts, solve(): returned.reshape(wide, span_wide, span_narrow, layers).transpose(1, 2, 0, 3)  13.9 us
    dot_general x2, matrix products, solve(): waves = jnp.einsum('xyz,zk->xyk', real_field, table, precision=highest)  10.2 us
  transfers between devices with their start and end apart: 6, of which 5 were waited for; matrix products, arithmetic and copies ran while one was open for 1% of the time, Pallas kernels for 0%

profile of v1, /device:TPU:0, one launch (start us, length us, event | category | flops | bytes accessed | tf_op | source)
XLA Modules:
  0.0 267.4 jit_solution(3255043422832968500)
XLA Ops:
  0.0 3.6 %fusion.18 = f32[32,64,256]{2,1,0:T(8,128)S(1)} fusion(f32[256,256,1]{1,0,2:T(8,128)} %constant.48, s32[32,64,256]{2,1,0:T(8,128)} %param.7), kind=kOutput, calls=%fused_computation.31 | convolution fusion | flops 1611137024 | bytes 4456448 | tf_op jit(solution)/shard_map/xyz,zk->xyk/dot_general | solution.py:194
  3.6 2.7 %copy.12 = f32[32,64,256]{1,2,0:T(8,128)} copy(f32[32,64,256]{2,1,0:T(8,128)S(1)} %fusion.18) | data formatting | bytes 4194304 | tf_op jit(solution)/shard_map/xyz,zk->xyk/dot_general | solution.py:194
  6.4 7.0 %copy.13 = f32[8,32,64,32]{3,2,1,0:T(8,128)} copy(f32[8,32,64,32]{2,3,0,1:T(8,128)} %bitcast.35) | data formatting | bytes 4194304 | tf_op jit(solution)/shard_map/transpose | solution.py:195
  13.4 7.5 %reshape.53 = f32[8,32,2048]{2,1,0:T(8,128)} reshape(f32[8,32,64,32]{3,2,1,0:T(8,128)} %copy.13) | data formatting | bytes 4194304 | tf_op jit(solution)/shard_map/reshape | solution.py:197
  20.8 5.3 %all-to-all-start = ((f32[8,32,2048]{2,1,0:T(8,128)}), f32[8,32,2048]{2,1,0:T(8,128)S(1)}, u32[]{:S(2)}, u32[]{:S(2)}) async-start(f32[8,32,2048]{2,1,0:T(8,128)} %reshape.53), calls=%async_computation | async-start | bytes 4194304 | tf_op jit(solution)/shard_map/all_to_all | solution.py:196
  26.2 0.8 broadcast_multiply_fusion.1
  26.9 25.9 %all-to-all-done = f32[8,32,2048]{2,1,0:T(8,128)S(1)} async-done(((f32[8,32,2048]{2,1,0:T(8,128)}), f32[8,32,2048]{2,1,0:T(8,128)S(1)}, u32[]{:S(2)}, u32[]{:S(2)}) %all-to-all-start) | async-done | bytes 2097184 | tf_op jit(solution)/shard_map/all_to_all | solution.py:196
  52.8 19.1 %lines.2 = f32[256,2048]{1,0:T(8,128)S(1)} custom-call(f32[256,2048]{1,0:T(8,128)S(1)} %bitcast.27, f32[256,256]{1,0:T(8,128)S(1)} %copy-done, f32[32,256]{1,0:T(8,128)S(1)} %get-tuple-element.24.decay, f32[32,256]{1,0:T(8,128)S(1)} %get-tuple-element.23.scale, f32[64,88]{1,0:T(8,128)S(1)} %copy-done.1, f32[8,64]{1,0:T(8,128)S(1)} %copy-done.2, ...), custom_call_target="tpu_custom_call" | custom-call | flops 536870912 | bytes 4194304 | tf_op jit(solution)/shard_map/lines/pallas_call | solution.py:167
  72.0 31.0 %all_to_all.20 = f32[8,32,2048]{2,1,0:T(8,128)S(1)} all-to-all(f32[8,32,2048]{2,1,0:T(8,128)S(1)} %bitcast.30), channel_id=1, replica_groups=mesh['wide'=8,'narrow'=4] {'wide'}, dimensions={0} | all-to-all | bytes 4194304 | tf_op jit(solution)/shard_map/all_to_all | solution.py:200
  102.9 4.8 %reshape.56 = f32[8,32,64,32]{3,2,1,0:T(8,128)} reshape(f32[8,32,2048]{2,1,0:T(8,128)S(1)} %all_to_all.20) | data formatting | bytes 4194304 | tf_op jit(solution)/shard_map/reshape | solution.py:203
  107.7 6.9 %copy.14 = f32[32,64,8,32]{1,3,2,0:T(8,128)} copy(f32[32,64,8,32]{3,1,0,2:T(8,128)} %bitcast.31) | data formatting | bytes 4194304 | tf_op jit(solution)/shard_map/transpose | solution.py:203
  114.6 9.0 %fusion.32 = f32[32,64,256]{2,1,0:T(8,128)S(1)} fusion(f32[32,64,256]{1,2,0:T(8,128)} %bitcast.36, f32[256,256,1]{1,0,2:T(8,128)S(1)} %copy-done.3), kind=kOutput, calls=%fused_computation.51 | convolution fusion | flops 1610612736 | bytes 4456448 | tf_op jit(solution)/shard_map/xyk,kz->xyz/dot_general | solution.py:204
  123.7 2.6 collective-permute-start.1
  126.3 4.0 %collective-permute-done = f32[2,64,256]{2,1,0:T(8,128)S(1)} collective-permute-done((f32[2,64,256]{2,1,0:T(8,128)S(1)}, f32[2,64,256]{2,1,0:T(8,128)S(1)}, u32[]{:S(2)}, u32[]{:S(2)}) %collective-permute-start) | collective-permute-done | bytes 131104 | tf_op jit(solution)/shard_map/ppermute | solution.py:214
  130.4 1.6 collective-permute-start.2
  132.1 2.2 collective-permute-start.3
  134.3 2.5 collective-permute-done.2
  137.5 0.9 fusion.27
  138.8 4.6 %fusion.26 = (f32[34,66,256]{2,1,0:T(8,128)S(1)}, f32[34,66,256]{2,1,0:T(8,128)S(1)}) fusion(f32[34,66,255]{2,1,0:T(8,128)S(1)} %get-tuple-element.8, f32[34,66,1]{2,1,0:T(8,128)S(1)} %get-tuple-element.10, f32[34,66,1]{2,1,0:T(8,128)S(1)} %get-tuple-element.9, f32[34,66,255]{2,1,0:T(8,128)S(1)} %get-tuple-element.7, ...), kind=kLoop, calls=%fused_computation.45 | loop fusion | flops 12638208 | bytes 16293888 | tf_op jit(solution)/shard_map/mul | solution.py:233
  143.5 0.9 fusion.30
  144.8 1.8 fusion.22
  146.6 6.5 %fusion.7 = f32[32,64,256]{1,2,0:T(8,128)} fusion(f32[256,256,1]{1,0,2:T(8,128)S(1)} %copy-done.3, f32[34,66,256]{2,1,0:T(8,128)S(1)} %get-tuple-element.16, f32[34,66,256]{2,1,0:T(8,128)S(1)} %get-tuple-element.15, f32[32,64,1]{2,1,0:T(8,128)S(1)} %get-tuple-element.12, f32[32,64,255]{2,1,0:T(8,128)S(1)} %get-tuple-element.14, ...), kind=kOutput, calls=%fused_computation.18 | convolution fusion | flops 1614807040 | bytes 17039360 | tf_op jit(solution)/shard_map/xyz,zk->xyk/dot_general | solution.py:194
  153.1 7.0 %copy.17 = f32[8,32,64,32]{3,2,1,0:T(8,128)} copy(f32[8,32,64,32]{2,3,0,1:T(8,128)} %bitcast.33) | data formatting | bytes 4194304 | tf_op jit(solution)/shard_map/transpose | solution.py:195
  160.1 7.5 %reshape.59 = f32[8,32,2048]{2,1,0:T(8,128)} reshape(f32[8,32,64,32]{3,2,1,0:T(8,128)} %copy.17) | data formatting | bytes 4194304 | tf_op jit(solution)/shard_map/reshape | solution.py:197
  167.6 3.6 %all-to-all-start.2 = ((f32[8,32,2048]{2,1,0:T(8,128)}), f32[8,32,2048]{2,1,0:T(8,128)S(1)}, u32[]{:S(2)}, u32[]{:S(2)}) async-start(f32[8,32,2048]{2,1,0:T(8,128)} %reshape.59), calls=%async_computation.2 | async-start | bytes 4194304 | tf_op jit(solution)/shard_map/all_to_all | solution.py:196
  171.2 0.8 broadcast_multiply_fusion
  172.0 25.8 %all-to-all-done.2 = f32[8,32,2048]{2,1,0:T(8,128)S(1)} async-done(((f32[8,32,2048]{2,1,0:T(8,128)}), f32[8,32,2048]{2,1,0:T(8,128)S(1)}, u32[]{:S(2)}, u32[]{:S(2)}) %all-to-all-start.2) | async-done | bytes 2097184 | tf_op jit(solution)/shard_map/all_to_all | solution.py:196
  197.8 18.6 %lines.3 = f32[256,2048]{1,0:T(8,128)S(1)} custom-call(f32[256,2048]{1,0:T(8,128)S(1)} %bitcast.28, f32[256,256]{1,0:T(8,128)S(1)} %copy-done, f32[32,256]{1,0:T(8,128)S(1)} %get-tuple-element.22.decay, f32[32,256]{1,0:T(8,128)S(1)} %get-tuple-element.21.scale, f32[64,88]{1,0:T(8,128)S(1)} %copy-done.1, f32[8,64]{1,0:T(8,128)S(1)} %copy-done.2, ...), custom_call_target="tpu_custom_call" | custom-call | flops 536870912 | bytes 4194304 | tf_op jit(solution)/shard_map/lines/pallas_call | solution.py:167
  216.4 29.1 %all_to_all.21 = f32[8,32,2048]{2,1,0:T(8,128)S(1)} all-to-all(f32[8,32,2048]{2,1,0:T(8,128)S(1)} %bitcast.29), channel_id=1, replica_groups=mesh['wide'=8,'narrow'=4] {'wide'}, dimensions={0} | all-to-all | bytes 4194304 | tf_op jit(solution)/shard_map/all_to_all | solution.py:200
  245.5 4.8 %reshape.62 = f32[8,32,64,32]{3,2,1,0:T(8,128)} reshape(f32[8,32,2048]{2,1,0:T(8,128)S(1)} %all_to_all.21) | data formatting | bytes 4194304 | tf_op jit(solution)/shard_map/reshape | solution.py:203
  250.2 7.0 %copy.18 = f32[32,64,8,32]{1,3,2,0:T(8,128)} copy(f32[32,64,8,32]{3,1,0,2:T(8,128)} %bitcast.32) | data formatting | bytes 4194304 | tf_op jit(solution)/shard_map/transpose | solution.py:203
  257.2 10.2 %convert_multiply_fusion = f32[32,64,256]{2,1,0:T(8,128)} fusion(s32[32,64,256]{2,1,0:T(8,128)S(1)} %copy-done.4, f32[32,64,256]{1,2,0:T(8,128)} %bitcast.34, f32[256,256,1]{1,0,2:T(8,128)S(1)} %copy-done.3), kind=kOutput, calls=%fused_computation.30 | convolution fusion | flops 1612709888 | bytes 6553600 | tf_op jit(solution)/shard_map/xyk,kz->xyz/dot_general | solution.py:204
  (20 shorter events, 1.7 us)
Async XLA Ops:
  20.8 32.0 %copy-start = (f32[256,256]{1,0:T(8,128)S(1)}, f32[256,256]{1,0:T(8,128)}, u32[]{:S(2)}) copy-start(f32[256,256]{1,0:T(8,128)} %constant.17.clone.table) | copy-start | bytes 786436
  20.8 32.0 %copy-start.1 = (f32[64,88]{1,0:T(8,128)S(1)}, f32[64,88]{1,0:T(8,128)}, u32[]{:S(2)}) copy-start(f32[64,88]{1,0:T(8,128)} %constant.44.clone.green) | copy-start | bytes 67588
  20.8 32.0 %copy-start.2 = (f32[8,64]{1,0:T(8,128)S(1)}, f32[8,64]{1,0:T(8,128)}, u32[]{:S(2)}) copy-start(f32[8,64]{1,0:T(8,128)} %constant.45.clone.moments) | copy-start | bytes 6148
  20.8 32.0 %all-to-all-start = ((f32[8,32,2048]{2,1,0:T(8,128)}), f32[8,32,2048]{2,1,0:T(8,128)S(1)}, u32[]{:S(2)}, u32[]{:S(2)}) async-start(f32[8,32,2048]{2,1,0:T(8,128)} %reshape.53), calls=%async_computation | async-start | bytes 4194304 | tf_op jit(solution)/shard_map/all_to_all | solution.py:196
  107.7 6.9 %copy-start.3 = (f32[256,256,1]{1,0,2:T(8,128)S(1)}, f32[256,256,1]{1,0,2:T(8,128)}, u32[]{:S(2)}) copy-start(f32[256,256,1]{1,0,2:T(8,128)} %constant.48) | copy-start | bytes 786436
  123.7 6.7 %collective-permute-start = (f32[2,64,256]{2,1,0:T(8,128)S(1)}, f32[2,64,256]{2,1,0:T(8,128)S(1)}, u32[]{:S(2)}, u32[]{:S(2)}) collective-permute-start(f32[2,64,256]{2,1,0:T(8,128)S(1)} %get-tuple-element.19), channel_id=1, source_target_pairs={{0,4},{4,8},{8,12},{12,16},{16,20},{20,24},{24,28},{28,0},{1,5},{5... | collective-permute-start | bytes 393224 | tf_op jit(solution)/shard_map/ppermute | solution.py:214
  123.7 6.6 %collective-permute-start.1 = (f32[2,64,256]{2,1,0:T(8,128)S(1)}, f32[2,64,256]{2,1,0:T(8,128)S(1)}, u32[]{:S(2)}, u32[]{:S(2)}) collective-permute-start(f32[2,64,256]{2,1,0:T(8,128)S(1)} %get-tuple-element.20), channel_id=1, source_target_pairs={{4,0},{8,4},{12,8},{16,12},{20,16},{24,20},{28,24},{0,28},{5,1},{9... | collective-permute-start | bytes 393224 | tf_op jit(solution)/shard_map/ppermute | solution.py:215
  130.4 6.4 %collective-permute-start.2 = (f32[36,2,256]{2,1,0:T(2,128)S(1)}, f32[36,2,256]{2,1,0:T(2,128)S(1)}, u32[]{:S(2)}, u32[]{:S(2)}) collective-permute-start(f32[36,2,256]{2,1,0:T(2,128)S(1)} %get-tuple-element.17), channel_id=1, source_target_pairs={{0,1},{1,2},{2,3},{3,0},{4,5},{5,6},{6,7},{7,4},{8,9},{9,10},{10,1... | collective-permute-start | bytes 221192 | tf_op jit(solution)/shard_map/ppermute | solution.py:214
  132.1 5.1 %collective-permute-start.3 = (f32[36,2,256]{2,1,0:T(2,128)S(1)}, f32[36,2,256]{2,1,0:T(2,128)S(1)}, u32[]{:S(2)}, u32[]{:S(2)}) collective-permute-start(f32[36,2,256]{2,1,0:T(2,128)S(1)} %get-tuple-element.18), channel_id=1, source_target_pairs={{1,0},{2,1},{3,2},{0,3},{5,4},{6,5},{7,6},{4,7},{9,8},{10,9},{11,1... | collective-permute-start | bytes 221192 | tf_op jit(solution)/shard_map/ppermute | solution.py:215
  167.6 30.2 %all-to-all-start.2 = ((f32[8,32,2048]{2,1,0:T(8,128)}), f32[8,32,2048]{2,1,0:T(8,128)S(1)}, u32[]{:S(2)}, u32[]{:S(2)}) async-start(f32[8,32,2048]{2,1,0:T(8,128)} %reshape.59), calls=%async_computation.2 | async-start | bytes 4194304 | tf_op jit(solution)/shard_map/all_to_all | solution.py:196
  250.2 7.0 %copy-start.4 = (s32[32,64,256]{2,1,0:T(8,128)S(1)}, s32[32,64,256]{2,1,0:T(8,128)}, u32[]{:S(2)}) copy-start(s32[32,64,256]{2,1,0:T(8,128)} %param.8) | copy-start | bytes 6291460

commit v2 on v1

--- a/solution.py
+++ b/solution.py
@@ -11,6 +11,7 @@
 
 highest = lax.Precision.HIGHEST
 moment_rows = 8
+lanes = 128
 
 
 def cas_table(length):
@@ -56,7 +57,6 @@
 
 def solve_kernel(n, field, table, decay, scale, green, moments, mask, out, work, sent, arrived, send_sem, recv_sem):
     span, layers, length = work.shape
-    lanes = 128
     group = lanes // layers
     chunks = span // group
     me = lax.axis_index("narrow")
@@ -67,9 +67,8 @@
         )
 
     def to_waves(c, carry):
-        columns = pl.ds(pl.multiple_of(c * lanes, lanes), lanes)
         block = lax.dot_general(
-            field[:, columns].T, table[...], (((1,), (0,)), ((), ())), precision=highest,
+            field[:, c].reshape(length, lanes).T, table[...], (((1,), (0,)), ((), ())), precision=highest,
             preferred_element_type=jnp.float32,
         )
         work[pl.ds(c * group, group)] = block.reshape(group, layers, length)
@@ -148,25 +147,26 @@
     work[:, 0, :] = work[:, 0, :] + extra
 
     def from_waves(c, carry):
-        columns = pl.ds(pl.multiple_of(c * lanes, lanes), lanes)
         block = work[pl.ds(c * group, group)].reshape(lanes, length)
-        out[:, columns] = lax.dot_general(
+        result = lax.dot_general(
             table[...], block, (((1,), (1,)), ((), ())), precision=highest, preferred_element_type=jnp.float32
         )
+        out[:, c] = result.reshape(out.shape[0], out.shape[2], lanes)
         return carry
 
     lax.fori_loop(0, chunks, from_waves, 0)
 
 
 def solve_lines(field, tables, decay, scale, mask, layers):
-    length, columns = field.shape
+    length = field.shape[0] * field.shape[2]
+    columns = field.shape[1] * lanes
     n = lax.axis_size("narrow")
     span = columns // layers
     rows = 2 * layers + moment_rows
     vmem = pl.BlockSpec(memory_space=pltpu.VMEM)
     return pl.pallas_call(
         partial(solve_kernel, n),
-        out_shape=jax.ShapeDtypeStruct((length, columns), jnp.float32),
+        out_shape=jax.ShapeDtypeStruct(field.shape, jnp.float32),
         in_specs=[vmem] * 7,
         out_specs=vmem,
         scratch_shapes=[
@@ -186,22 +186,107 @@
     )(field, tables[0], decay, scale, tables[1], tables[2], mask)
 
 
-def solve(real_field, tables, decay, scale, mask):
+def split_kernel(field, table, blocks, waves):
+    xs, span, length = field.shape
+    wide = blocks.shape[0]
+    layers = length // wide
+    group = lanes // layers
+    halves = length // lanes
+    step = max(1, 256 // span)
+
+    def transform(c, carry):
+        rows = field[pl.ds(c * step, step)].astype(jnp.float32).reshape(step * span, length)
+        result = jnp.dot(rows, table[...], precision=highest, preferred_element_type=jnp.float32)
+        start = pl.multiple_of(c * step * span, step * span)
+        for h in range(halves):
+            waves[h, pl.ds(start, step * span), :] = result[:, h * lanes : (h + 1) * lanes]
+        return carry
+
+    lax.fori_loop(0, xs // step, transform, 0)
+    slot_of = lax.broadcasted_iota(jnp.int32, (xs, lanes), 1) // layers
+
+    def place(g, carry):
+        for h in range(halves):
+            pieces = [waves[h, pl.ds(g * group + i, xs, stride=span), :] for i in range(group)]
+            for slot in range(group):
+                total = None
+                for i in range(group):
+                    shift = ((i - slot) * layers) % lanes
+                    moved = pltpu.roll(pieces[i], shift, 1) if shift else pieces[i]
+                    total = moved if total is None else jnp.where(slot_of == i, moved, total)
+                blocks[h * group + slot, g] = total
+        return carry
+
+    lax.fori_loop(0, span // group, place, 0)
+
+
+def join_kernel(signed, blocks, table, *rest):
+    labels = rest[0] if signed else None
+    field, waves = rest[-2:]
+    xs, span, length = field.shape
+    wide = blocks.shape[0]
+    layers = length // wide
+    group = lanes // layers
+    halves = length // lanes
+    step = max(1, 256 // span)
+    slot_of = lax.broadcasted_iota(jnp.int32, (xs, lanes), 1) // layers
+
+    def place(g, carry):
+        for h in range(halves):
+            pieces = [blocks[h * group + slot, g] for slot in range(group)]
+            for i in range(group):
+                total = None
+                for slot in range(group):
+                    shift = ((slot - i) * layers) % lanes
+                    moved = pltpu.roll(pieces[slot], shift, 1) if shift else pieces[slot]
+                    total = moved if total is None else jnp.where(slot_of == slot, moved, total)
+                waves[h, pl.ds(g * group + i, xs, stride=span), :] = total
+        return carry
+
+    lax.fori_loop(0, span // group, place, 0)
+
+    def transform(c, carry):
+        start = pl.multiple_of(c * step * span, step * span)
+        rows = jnp.concatenate([waves[h, pl.ds(start, step * span), :] for h in range(halves)], axis=1)
+        result = jnp.dot(rows, table[...], precision=highest, preferred_element_type=jnp.float32)
+        result = result.reshape(step, span, length)
+        if signed:
+            result = result * (2 * labels[pl.ds(c * step, step)] - 1).astype(jnp.float32)
+        field[pl.ds(c * step, step)] = result
+        return carry
+
+    lax.fori_loop(0, xs // step, transform, 0)
+
+
+def local_call(kernel, args, shape, rows, length, name):
+    vmem = pl.BlockSpec(memory_space=pltpu.VMEM)
+    return pl.pallas_call(
+        kernel,
+        out_shape=jax.ShapeDtypeStruct(shape, jnp.float32),
+        in_specs=[vmem] * len(args),
+        out_specs=vmem,
+        scratch_shapes=[pltpu.VMEM((length // lanes, rows, lanes), jnp.float32)],
+        compiler_params=pltpu.CompilerParams(vmem_limit_bytes=40 * 1024 * 1024),
+        cost_estimate=pl.CostEstimate(
+            flops=2 * rows * length * length, bytes_accessed=8 * rows * length, transcendentals=0
+        ),
+        name=name,
+    )(*args)
+
+
+def solve(real_field, tables, decay, scale, mask, labels=None):
     table = tables[0]
-    span_wide, span_narrow, length = real_field.shape
+    xs, span, length = real_field.shape
     wide = lax.axis_size("wide")
     layers = length // wide
-    waves = jnp.einsum("xyz,zk->xyk", real_field, table, precision=highest)
-    blocks = waves.reshape(span_wide, span_narrow, wide, layers).transpose(2, 0, 1, 3)
-    arrived = lax.all_to_all(
-        blocks.reshape(wide, span_wide, span_narrow * layers), "wide", split_axis=0, concat_axis=0, tiled=True
-    )
-    lines = solve_lines(arrived.reshape(length, span_narrow * layers), tables, decay, scale, mask, layers)
-    returned = lax.all_to_all(
-        lines.reshape(wide, span_wide, span_narrow * layers), "wide", split_axis=0, concat_axis=0, tiled=True
-    )
-    waves = returned.reshape(wide, span_wide, span_narrow, layers).transpose(1, 2, 0, 3)
-    return jnp.einsum("xyk,kz->xyz", waves.reshape(span_wide, span_narrow, length), table, precision=highest)
+    shape = (wide, span * layers // lanes, xs, lanes)
+    blocks = local_call(split_kernel, (real_field, table), shape, xs * span, length, "split")
+    blocks = lax.all_to_all(blocks, "wide", split_axis=0, concat_axis=0, tiled=True)
+    blocks = solve_lines(blocks, tables, decay, scale, mask, layers)
+    blocks = lax.all_to_all(blocks, "wide", split_axis=0, concat_axis=0, tiled=True)
+    args = (blocks, table) if labels is None else (blocks, table, labels)
+    kernel = partial(join_kernel, labels is not None)
+    return local_call(kernel, args, real_field.shape, xs * span, length, "join")
 
 
 def extended(x, sides, width):
@@ -256,15 +341,13 @@
     corner = (jnp.arange(length, dtype=jnp.int32)[None, :] == 0) & (place == 0)
     norm = float(length) ** 2
     heat_field = solve(
-        sources.astype(jnp.float32), tables, heat_decay, heat_decay * (1.0 / (heat_time * norm)),
+        sources, tables, heat_decay, heat_decay * (1.0 / (heat_time * norm)),
         jnp.zeros((1, length), jnp.float32),
     )
     divergence = flow_divergence(heat_field, grad_floor)
-    potential = solve(
-        divergence, tables, line_decay, line_decay * (-1.0 / norm), jnp.where(corner, -1.0 / norm, 0.0)
+    return solve(
+        divergence, tables, line_decay, line_decay * (-1.0 / norm), jnp.where(corner, -1.0 / norm, 0.0), labels
     )
-    signs = (2 * labels - 1).astype(jnp.float32)
-    return signs * potential
 
 
 def solution(mesh):

time: 268 us -> 217 us (0.81)
  local copies, waits for them, and re-layouts: 57.7 us -> 7.72 us
  matrix products: 29.4 us -> 0 us
  Pallas kernels: 37.7 us -> 64.7 us
    dot_general x4 -> x0, matrix products: 29.4 us -> none  [the longest x2 19.2 us: solve(): jnp.einsum('xyk,kz->xyz', waves.reshape(span_wide, span_narrow, length),...]
    transpose x4 -> x0, local copies, waits for them, and re-layouts: 27.8 us -> none  [the longest x2 13.9 us: solve(): waves.reshape(span_wide, span_narrow, wide, layers).transpose(2, 0, 1, 3)]
    pallas_call x2 -> x6, Pallas kernels: 37.7 us -> 64.7 us  [the longest x2 37.6 us: solve_lines(): pl.pallas_call(partial(solve_kernel, n), out_shape=jax.ShapeDtypeStruct(f...]
    reshape x4 -> x0, local copies, waits for them, and re-layouts: 24.5 us -> none  [the longest x2 15 us: solve(): blocks.reshape(wide, span_wide, span_narrow * layers)]
    unnamed x10 -> x16, local copies, waits for them, and re-layouts: 0.02 us -> 5.18 us
    dot_general x1 -> x0, local copies, waits for them, and re-layouts: 2.75 us -> none  [solve(): waves = jnp.einsum('xyz,zk->xyk', real_field, table, precision=highest)]
where the time goes in v2:
time: 217 us
  Pallas kernels  64.7 us (30%)
  blocking collectives  60.2 us (28%)
  waiting for transfers between devices  58.6 us (27%)
  starting transfers between devices  15.5 us (7%)
  other arithmetic  9.66 us (4%)
  local copies, waits for them, and re-layouts  7.72 us (4%)
    all_to_all x2, blocking collectives, solve(): lax.all_to_all(blocks, 'wide', split_axis=0, concat_axis=0, tiled=True)  60.2 us
    all_to_all x2, waiting for transfers between devices, solve(): lax.all_to_all(blocks, 'wide', split_axis=0, concat_axis=0, tiled=True)  51.7 us
    pallas_call x2, Pallas kernels, solve_lines(): pl.pallas_call(partial(solve_kernel, n), out_shape=jax.ShapeDtypeStruct(f...  37.6 us
    pallas_call x4, Pallas kernels, local_call(): pl.pallas_call(kernel, out_shape=jax.ShapeDtypeStruct(shape, jnp.float32)...  27.1 us
    all_to_all x2, starting transfers between devices, solve(): lax.all_to_all(blocks, 'wide', split_axis=0, concat_axis=0, tiled=True)  8.91 us
    ppermute x2, waiting for transfers between devices, extended(): before = lax.ppermute(last, axis, up)  6.46 us
    unnamed x16, local copies, waits for them, and re-layouts  5.18 us
    ppermute x2, starting transfers between devices, extended(): after = lax.ppermute(initial, axis, down)  4.88 us
  transfers between devices with their start and end apart: 6, of which 5 were waited for; matrix products, arithmetic and copies ran while one was open for 1% of the time, Pallas kernels for 0%

profile of v2, /device:TPU:0, one launch (start us, length us, event | category | flops | bytes accessed | tf_op | source)
XLA Modules:
  0.0 216.5 jit_solution(8458846790060537045)
XLA Ops:
  0.0 0.9 copy-done
  1.0 1.6 copy-done.5
  2.5 6.2 %split.2 = f32[8,16,32,128]{3,2,1,0:T(8,128)S(1)} custom-call(s32[32,64,256]{2,1,0:T(8,128)S(1)} %copy-done.5, f32[256,256]{1,0:T(8,128)S(1)} %copy-done), custom_call_target="tpu_custom_call" | custom-call | flops 268435456 | bytes 4194304 | tf_op jit(solution)/shard_map/split/pallas_call | solution.py:263
  8.7 1.3 copy-done.2
  10.0 5.3 %all-to-all-start = ((f32[8,16,32,128]{3,2,1,0:T(8,128)}), f32[8,16,32,128]{3,2,1,0:T(8,128)S(1)}, u32[]{:S(2)}, u32[]{:S(2)}) async-start(f32[8,16,32,128]{3,2,1,0:T(8,128)} %copy-done.2), calls=%async_computation | async-start | bytes 4194304 | tf_op jit(solution)/shard_map/all_to_all | solution.py:284
  15.3 0.8 broadcast_multiply_fusion.1
  16.1 25.9 %all-to-all-done.field = f32[8,16,32,128]{3,2,1,0:T(8,128)S(1)} async-done(((f32[8,16,32,128]{3,2,1,0:T(8,128)}), f32[8,16,32,128]{3,2,1,0:T(8,128)S(1)}, u32[]{:S(2)}, u32[]{:S(2)}) %all-to-all-start) | async-done | bytes 2097184 | tf_op jit(solution)/shard_map/all_to_all | solution.py:284
  42.0 19.0 %lines.2 = f32[8,16,32,128]{3,2,1,0:T(8,128)S(1)} custom-call(f32[8,16,32,128]{3,2,1,0:T(8,128)S(1)} %all-to-all-done.field, f32[256,256]{1,0:T(8,128)S(1)} %copy-done.1, f32[32,256]{1,0:T(8,128)S(1)} %get-tuple-element.24.decay, f32[32,256]{1,0:T(8,128)S(1)} %get-tuple-element.23.scale, f32[64,88]{1,0:T(8,128)S(1)} %copy-done.6, f32[8,64]{1,0:T(8,128)S(1)} %copy-done.7, ...), custom_call_target="tpu_custom_call" | custom-call | flops 536870912 | bytes 4194304 | tf_op jit(solution)/shard_map/lines/pallas_call | solution.py:167
  61.0 31.0 %all_to_all.20.blocks = f32[8,16,32,128]{3,2,1,0:T(8,128)S(1)} all-to-all(f32[8,16,32,128]{3,2,1,0:T(8,128)S(1)} %lines.2), channel_id=1, replica_groups=mesh['wide'=8,'narrow'=4] {'wide'}, dimensions={0} | all-to-all | bytes 4194304 | tf_op jit(solution)/shard_map/all_to_all | solution.py:286
  92.1 6.7 %join.2 = f32[32,64,256]{2,1,0:T(8,128)S(1)} custom-call(f32[8,16,32,128]{3,2,1,0:T(8,128)S(1)} %all_to_all.20.blocks, f32[256,256]{1,0:T(8,128)S(1)} %copy-done.1), custom_call_target="tpu_custom_call" | custom-call | flops 268435456 | bytes 4194304 | tf_op jit(solution)/shard_map/join/pallas_call | solution.py:263
  98.9 2.6 %collective-permute-start.1 = (f32[2,64,256]{2,1,0:T(8,128)S(1)}, f32[2,64,256]{2,1,0:T(8,128)S(1)}, u32[]{:S(2)}, u32[]{:S(2)}) collective-permute-start(f32[2,64,256]{2,1,0:T(8,128)S(1)} %get-tuple-element.20), channel_id=1, source_target_pairs={{4,0},{8,4},{12,8},{16,12},{20,16},{24,20},{28,24},{0,28},{5,1},{9... | collective-permute-start | bytes 393224 | tf_op jit(solution)/shard_map/ppermute | solution.py:300
  101.5 4.0 %collective-permute-done = f32[2,64,256]{2,1,0:T(8,128)S(1)} collective-permute-done((f32[2,64,256]{2,1,0:T(8,128)S(1)}, f32[2,64,256]{2,1,0:T(8,128)S(1)}, u32[]{:S(2)}, u32[]{:S(2)}) %collective-permute-start) | collective-permute-done | bytes 131104 | tf_op jit(solution)/shard_map/ppermute | solution.py:299
  105.6 1.6 collective-permute-start.2
  107.2 2.2 %collective-permute-start.3 = (f32[36,2,256]{2,1,0:T(2,128)S(1)}, f32[36,2,256]{2,1,0:T(2,128)S(1)}, u32[]{:S(2)}, u32[]{:S(2)}) collective-permute-start(f32[36,2,256]{2,1,0:T(2,128)S(1)} %get-tuple-element.18), channel_id=1, source_target_pairs={{1,0},{2,1},{3,2},{0,3},{5,4},{6,5},{7,6},{4,7},{9,8},{10,9},{11,1... | collective-permute-start | bytes 221192 | tf_op jit(solution)/shard_map/ppermute | solution.py:300
  109.5 2.5 %collective-permute-done.2 = f32[36,2,256]{2,1,0:T(2,128)S(1)} collective-permute-done((f32[36,2,256]{2,1,0:T(2,128)S(1)}, f32[36,2,256]{2,1,0:T(2,128)S(1)}, u32[]{:S(2)}, u32[]{:S(2)}) %collective-permute-start.2) | collective-permute-done | bytes 73760 | tf_op jit(solution)/shard_map/ppermute | solution.py:299
  111.9 0.4 collective-permute-done.3
  112.4 0.3 pad_maximum_fusion
  112.7 0.9 fusion.10
  113.6 0.4 fusion.11
  114.0 4.6 %fusion.9 = (f32[34,66,256]{2,1,0:T(8,128)S(1)}, f32[34,66,256]{2,1,0:T(8,128)S(1)}) fusion(f32[34,66,255]{2,1,0:T(8,128)S(1)} %get-tuple-element.8, f32[34,66,1]{2,1,0:T(8,128)S(1)} %get-tuple-element.10, f32[34,66,1]{2,1,0:T(8,128)S(1)} %get-tuple-element.9, f32[34,66,255]{2,1,0:T(8,128)S(1)} %get-tuple-element.7, ...), kind=kLoop, calls=%fused_computation.30 | loop fusion | flops 12638208 | bytes 16293888 | tf_op jit(solution)/shard_map/mul | solution.py:318
  118.6 0.8 fusion.13
  119.4 0.4 fusion.12
  119.9 1.9 fusion.7
  121.8 1.2 fusion.6.field
  123.0 6.1 %split.3 = f32[8,16,32,128]{3,2,1,0:T(8,128)S(1)} custom-call(f32[32,64,256]{2,1,0:T(8,128)S(1)} %fusion.6.field, f32[256,256]{1,0:T(8,128)S(1)} %copy-done.1), custom_call_target="tpu_custom_call" | custom-call | flops 268435456 | bytes 4194304 | tf_op jit(solution)/shard_map/split/pallas_call | solution.py:263
  129.1 1.3 copy-done.3
  130.4 3.6 %all-to-all-start.2 = ((f32[8,16,32,128]{3,2,1,0:T(8,128)}), f32[8,16,32,128]{3,2,1,0:T(8,128)S(1)}, u32[]{:S(2)}, u32[]{:S(2)}) async-start(f32[8,16,32,128]{3,2,1,0:T(8,128)} %copy-done.3), calls=%async_computation.2 | async-start | bytes 4194304 | tf_op jit(solution)/shard_map/all_to_all | solution.py:284
  134.1 0.8 broadcast_multiply_fusion
  134.8 25.8 %all-to-all-done.2.field = f32[8,16,32,128]{3,2,1,0:T(8,128)S(1)} async-done(((f32[8,16,32,128]{3,2,1,0:T(8,128)}), f32[8,16,32,128]{3,2,1,0:T(8,128)S(1)}, u32[]{:S(2)}, u32[]{:S(2)}) %all-to-all-start.2) | async-done | bytes 2097184 | tf_op jit(solution)/shard_map/all_to_all | solution.py:284
  160.6 18.5 %lines.3 = f32[8,16,32,128]{3,2,1,0:T(8,128)S(1)} custom-call(f32[8,16,32,128]{3,2,1,0:T(8,128)S(1)} %all-to-all-done.2.field, f32[256,256]{1,0:T(8,128)S(1)} %copy-done.1, f32[32,256]{1,0:T(8,128)S(1)} %get-tuple-element.22.decay, f32[32,256]{1,0:T(8,128)S(1)} %get-tuple-element.21.scale, f32[64,88]{1,0:T(8,128)S(1)} %copy-done.6, f32[8,64]{1,0:T(8,128)S(1)} %copy-done.7, ...), custom_call_target="tpu_custom_call" | custom-call | flops 536870912 | bytes 4194304 | tf_op jit(solution)/shard_map/lines/pallas_call | solution.py:167
  179.2 29.2 %all_to_all.21.blocks = f32[8,16,32,128]{3,2,1,0:T(8,128)S(1)} all-to-all(f32[8,16,32,128]{3,2,1,0:T(8,128)S(1)} %lines.3), channel_id=1, replica_groups=mesh['wide'=8,'narrow'=4] {'wide'}, dimensions={0} | all-to-all | bytes 4194304 | tf_op jit(solution)/shard_map/all_to_all | solution.py:286
  208.4 8.1 %join.3 = f32[32,64,256]{2,1,0:T(8,128)} custom-call(f32[8,16,32,128]{3,2,1,0:T(8,128)S(1)} %all_to_all.21.blocks, f32[256,256]{1,0:T(8,128)S(1)} %copy-done.1, s32[32,64,256]{2,1,0:T(8,128)S(1)} %copy-done.4), custom_call_target="tpu_custom_call" | custom-call | flops 268435456 | bytes 4194304 | tf_op jit(solution)/shard_map/join/pallas_call | solution.py:263
  (18 shorter events, 0.2 us)
Async XLA Ops:
  0.0 0.9 copy-start
  1.0 1.6 copy-start.5
  8.7 1.3 copy-start.2
  10.0 32.0 %copy-start.1 = (f32[256,256]{1,0:T(8,128)S(1)}, f32[256,256]{1,0:T(8,128)}, u32[]{:S(2)}) copy-start(f32[256,256]{1,0:T(8,128)} %constant.14.clone.table) | copy-start | bytes 786436
  10.0 32.0 %copy-start.6 = (f32[64,88]{1,0:T(8,128)S(1)}, f32[64,88]{1,0:T(8,128)}, u32[]{:S(2)}) copy-start(f32[64,88]{1,0:T(8,128)} %constant.15.clone.green) | copy-start | bytes 67588
  10.0 32.0 %copy-start.7 = (f32[8,64]{1,0:T(8,128)S(1)}, f32[8,64]{1,0:T(8,128)}, u32[]{:S(2)}) copy-start(f32[8,64]{1,0:T(8,128)} %constant.40.clone.moments) | copy-start | bytes 6148
  10.0 31.9 %all-to-all-start = ((f32[8,16,32,128]{3,2,1,0:T(8,128)}), f32[8,16,32,128]{3,2,1,0:T(8,128)S(1)}, u32[]{:S(2)}, u32[]{:S(2)}) async-start(f32[8,16,32,128]{3,2,1,0:T(8,128)} %copy-done.2), calls=%async_computation | async-start | bytes 4194304 | tf_op jit(solution)/shard_map/all_to_all | solution.py:284
  98.8 6.7 %collective-permute-start = (f32[2,64,256]{2,1,0:T(8,128)S(1)}, f32[2,64,256]{2,1,0:T(8,128)S(1)}, u32[]{:S(2)}, u32[]{:S(2)}) collective-permute-start(f32[2,64,256]{2,1,0:T(8,128)S(1)} %get-tuple-element.19), channel_id=1, source_target_pairs={{0,4},{4,8},{8,12},{12,16},{16,20},{20,24},{24,28},{28,0},{1,5},{5... | collective-permute-start | bytes 393224 | tf_op jit(solution)/shard_map/ppermute | solution.py:299
  98.9 6.6 %collective-permute-start.1 = (f32[2,64,256]{2,1,0:T(8,128)S(1)}, f32[2,64,256]{2,1,0:T(8,128)S(1)}, u32[]{:S(2)}, u32[]{:S(2)}) collective-permute-start(f32[2,64,256]{2,1,0:T(8,128)S(1)} %get-tuple-element.20), channel_id=1, source_target_pairs={{4,0},{8,4},{12,8},{16,12},{20,16},{24,20},{28,24},{0,28},{5,1},{9... | collective-permute-start | bytes 393224 | tf_op jit(solution)/shard_map/ppermute | solution.py:300
  105.6 6.3 %collective-permute-start.2 = (f32[36,2,256]{2,1,0:T(2,128)S(1)}, f32[36,2,256]{2,1,0:T(2,128)S(1)}, u32[]{:S(2)}, u32[]{:S(2)}) collective-permute-start(f32[36,2,256]{2,1,0:T(2,128)S(1)} %get-tuple-element.17), channel_id=1, source_target_pairs={{0,1},{1,2},{2,3},{3,0},{4,5},{5,6},{6,7},{7,4},{8,9},{9,10},{10,1... | collective-permute-start | bytes 221192 | tf_op jit(solution)/shard_map/ppermute | solution.py:299
  107.2 5.1 %collective-permute-start.3 = (f32[36,2,256]{2,1,0:T(2,128)S(1)}, f32[36,2,256]{2,1,0:T(2,128)S(1)}, u32[]{:S(2)}, u32[]{:S(2)}) collective-permute-start(f32[36,2,256]{2,1,0:T(2,128)S(1)} %get-tuple-element.18), channel_id=1, source_target_pairs={{1,0},{2,1},{3,2},{0,3},{5,4},{6,5},{7,6},{4,7},{9,8},{10,9},{11,1... | collective-permute-start | bytes 221192 | tf_op jit(solution)/shard_map/ppermute | solution.py:300
  129.1 1.3 copy-start.3
  130.4 30.2 %all-to-all-start.2 = ((f32[8,16,32,128]{3,2,1,0:T(8,128)}), f32[8,16,32,128]{3,2,1,0:T(8,128)S(1)}, u32[]{:S(2)}, u32[]{:S(2)}) async-start(f32[8,16,32,128]{3,2,1,0:T(8,128)} %copy-done.3), calls=%async_computation.2 | async-start | bytes 4194304 | tf_op jit(solution)/shard_map/all_to_all | solution.py:284
  179.2 29.2 %copy-start.4 = (s32[32,64,256]{2,1,0:T(8,128)S(1)}, s32[32,64,256]{2,1,0:T(8,128)}, u32[]{:S(2)}) copy-start(s32[32,64,256]{2,1,0:T(8,128)} %rest_0_.1) | copy-start | bytes 6291460

commit v3 on v1

--- a/solution.py
+++ b/solution.py
@@ -11,6 +11,7 @@
 
 highest = lax.Precision.HIGHEST
 moment_rows = 8
+lanes = 128
 
 
 def cas_table(length):
@@ -54,30 +55,111 @@
     return result
 
 
-def solve_kernel(n, field, table, decay, scale, green, moments, mask, out, work, sent, arrived, send_sem, recv_sem):
-    span, layers, length = work.shape
-    lanes = 128
+def solve_kernel(n, signed, field, table, decay, scale, green, moments, mask, *rest):
+    labels = rest[0] if signed else None
+    out, waves, work, outgoing, incoming, sent, arrived, send_sem, recv_sem, wide_send, wide_recv = rest[1:] if signed else rest
+    xs, span, length = field.shape
+    wide = incoming.shape[1]
+    layers = length // wide
     group = lanes // layers
+    halves = length // lanes
     chunks = span // group
+    parts = wide_send.shape[1]
+    each = chunks // parts
+    rows_each = span // parts
+    step_rows = max(1, 256 // span)
     me = lax.axis_index("narrow")
+    here = lax.axis_index("wide")
+    mesh_ids = pl.DeviceIdType.MESH
     barrier = pltpu.get_barrier_semaphore()
     for step in range(1, n):
-        pl.semaphore_signal(
-            barrier, inc=1, device_id={"narrow": lax.rem(me + step, n)}, device_id_type=pl.DeviceIdType.MESH
+        pl.semaphore_signal(barrier, inc=1, device_id={"narrow": lax.rem(me + step, n)}, device_id_type=mesh_ids)
+
+    def greet(step, carry):
+        pl.semaphore_signal(barrier, inc=1, device_id={"wide": lax.rem(here + step, wide)}, device_id_type=mesh_ids)
+        return carry
+
+    lax.fori_loop(1, wide, greet, 0)
+
+    def block_copy(turn, part, step):
+        target = lax.rem(here + step, wide)
+        some = pl.ds(part * each, each)
+        return pltpu.make_async_remote_copy(
+            src_ref=outgoing.at[turn, target, some],
+            dst_ref=incoming.at[turn, here, some],
+            send_sem=wide_send.at[turn, part, step],
+            recv_sem=wide_recv.at[turn, part, step],
+            device_id={"wide": target},
+            device_id_type=mesh_ids,
         )
 
+    def send_part(turn, part):
+        def one(step, carry):
+            block_copy(turn, part, step).start()
+            return carry
+
+        lax.fori_loop(1, wide, one, 0)
+        some = pl.ds(part * each, each)
+        incoming[turn, here, some] = outgoing[turn, here, some]
+
+    def receive_part(turn, part):
+        def one(step, carry):
+            block_copy(turn, part, step).wait_recv()
+            return carry
+
+        lax.fori_loop(1, wide, one, 0)
+
+    def finish_part(turn, part):
+        def one(step, carry):
+            block_copy(turn, part, step).wait_send()
+            return carry
+
+        lax.fori_loop(1, wide, one, 0)
+
+    def transform(c, carry):
+        rows = field[pl.ds(c * step_rows, step_rows)].astype(jnp.float32).reshape(step_rows * span, length)
+        result = jnp.dot(rows, table[...], precision=highest, preferred_element_type=jnp.float32)
+        start = pl.multiple_of(c * step_rows * span, step_rows * span)
+        for h in range(halves):
+            waves[h, pl.ds(start, step_rows * span), :] = result[:, h * lanes : (h + 1) * lanes]
+        return carry
+
+    lax.fori_loop(0, xs // step_rows, transform, 0)
+    slot_of = lax.broadcasted_iota(jnp.int32, (xs, lanes), 1) // layers
+
+    def split(g, carry):
+        for h in range(halves):
+            pieces = [waves[h, pl.ds(g * group + i, xs, stride=span), :] for i in range(group)]
+            for slot in range(group):
+                total = None
+                for i in range(group):
+                    shift = ((i - slot) * layers) % lanes
+                    moved = pltpu.roll(pieces[i], shift, 1) if shift else pieces[i]
+                    total = moved if total is None else jnp.where(slot_of == i, moved, total)
+                outgoing[0, h * group + slot, g] = total
+        return carry
+
+    for part in range(parts):
+        lax.fori_loop(part * each, (part + 1) * each, split, 0)
+        if part == 0:
+            pl.semaphore_wait(barrier, n - 1 + wide - 1)
+        send_part(0, part)
+
+    r = decay[...]
+    s = scale[...]
+
     def to_waves(c, carry):
-        columns = pl.ds(pl.multiple_of(c * lanes, lanes), lanes)
         block = lax.dot_general(
-            field[:, columns].T, table[...], (((1,), (0,)), ((), ())), precision=highest,
+            incoming[0, :, c].reshape(length, lanes).T, table[...], (((1,), (0,)), ((), ())), precision=highest,
             preferred_element_type=jnp.float32,
         )
         work[pl.ds(c * group, group)] = block.reshape(group, layers, length)
         return carry
 
-    lax.fori_loop(0, chunks, to_waves, 0)
-    r = decay[...]
-    s = scale[...]
+    for part in range(parts):
+        receive_part(0, part)
+        lax.fori_loop(part * each, (part + 1) * each, to_waves, 0)
+
     column = work[:, 0, :]
     sent[2 * layers :, :] = jnp.dot(moments[...], column, precision=highest, preferred_element_type=jnp.float32)
 
@@ -97,7 +179,6 @@
     u_first = lax.fori_loop(0, span, back, jnp.zeros_like(r), unroll=4)
     sent[0:layers, :] = v_last
     sent[layers : 2 * layers, :] = u_first
-    pl.semaphore_wait(barrier, n - 1)
     copies = []
     for step in range(1, n):
         copy = pltpu.make_async_remote_copy(
@@ -106,21 +187,23 @@
             send_sem=send_sem.at[step - 1],
             recv_sem=recv_sem.at[n - 1 - step],
             device_id={"narrow": lax.rem(me + step, n)},
-            device_id_type=pl.DeviceIdType.MESH,
+            device_id_type=mesh_ids,
         )
         copy.start()
         copies.append(copy)
+    for part in range(parts):
+        finish_part(0, part)
+    q = power(r, span)
+    close = 1.0 / (1.0 - power(q, n))
+    factor = s / (1.0 - r * r)
+    tail = q * r
+    edge = r - tail * q
     for copy in copies:
         copy.wait()
     stacked = jnp.concatenate([column] + [arrived[d, 2 * layers :, :] for d in range(n - 1)], axis=0)
     extra = jnp.dot(green[...], stacked, precision=highest, preferred_element_type=jnp.float32) * mask[...]
     last = [v_last] + [arrived[d, 0:layers, :] for d in range(n - 1)]
     first = [u_first] + [arrived[d, layers : 2 * layers, :] for d in range(n - 1)]
-    q = power(r, span)
-    close = 1.0 / (1.0 - power(q, n))
-    factor = s / (1.0 - r * r)
-    tail = q * r
-    edge = r - tail * q
     alphas = []
     for t in range(n):
         total = last[t % n]
@@ -138,70 +221,94 @@
         return p * r
 
     lax.fori_loop(0, span, add_ahead, alphas[0] * r, unroll=4)
+    work[:, 0, :] = work[:, 0, :] + extra
 
     def add_back(i, p):
         j = span - 1 - i
         work[j] = work[j] + p
         return p * r
 
-    lax.fori_loop(0, span, add_back, (inflow - alphas[0] * tail) * r, unroll=4)
-    work[:, 0, :] = work[:, 0, :] + extra
-
     def from_waves(c, carry):
-        columns = pl.ds(pl.multiple_of(c * lanes, lanes), lanes)
         block = work[pl.ds(c * group, group)].reshape(lanes, length)
-        out[:, columns] = lax.dot_general(
+        result = lax.dot_general(
             table[...], block, (((1,), (1,)), ((), ())), precision=highest, preferred_element_type=jnp.float32
         )
-        return carry
-
-    lax.fori_loop(0, chunks, from_waves, 0)
-
-
-def solve_lines(field, tables, decay, scale, mask, layers):
-    length, columns = field.shape
+        outgoing[1, :, c] = result.reshape(wide, xs, lanes)
+        return carry
+
+    p = (inflow - alphas[0] * tail) * r
+    for turn in range(parts):
+        part = parts - 1 - turn
+        p = lax.fori_loop(turn * rows_each, (turn + 1) * rows_each, add_back, p, unroll=4)
+        lax.fori_loop(part * each, (part + 1) * each, from_waves, 0)
+        send_part(1, part)
+
+    def join(g, carry):
+        for h in range(halves):
+            pieces = [incoming[1, h * group + slot, g] for slot in range(group)]
+            for i in range(group):
+                total = None
+                for slot in range(group):
+                    shift = ((slot - i) * layers) % lanes
+                    moved = pltpu.roll(pieces[slot], shift, 1) if shift else pieces[slot]
+                    total = moved if total is None else jnp.where(slot_of == slot, moved, total)
+                waves[h, pl.ds(g * group + i, xs, stride=span), :] = total
+        return carry
+
+    for part in reversed(range(parts)):
+        receive_part(1, part)
+        lax.fori_loop(part * each, (part + 1) * each, join, 0)
+
+    def transform_back(c, carry):
+        start = pl.multiple_of(c * step_rows * span, step_rows * span)
+        rows = jnp.concatenate([waves[h, pl.ds(start, step_rows * span), :] for h in range(halves)], axis=1)
+        result = jnp.dot(rows, table[...], precision=highest, preferred_element_type=jnp.float32)
+        result = result.reshape(step_rows, span, length)
+        if signed:
+            result = result * (2 * labels[pl.ds(c * step_rows, step_rows)] - 1).astype(jnp.float32)
+        out[pl.ds(c * step_rows, step_rows)] = result
+        return carry
+
+    lax.fori_loop(0, xs // step_rows, transform_back, 0)
+    for part in range(parts):
+        finish_part(1, part)
+
+
+def solve(real_field, tables, decay, scale, mask, labels=None):
+    xs, span, length = real_field.shape
     n = lax.axis_size("narrow")
-    span = columns // layers
+    wide = lax.axis_size("wide")
+    layers = length // wide
+    chunks = span * layers // lanes
+    parts = min(4, chunks)
     rows = 2 * layers + moment_rows
     vmem = pl.BlockSpec(memory_space=pltpu.VMEM)
+    args = (real_field, tables[0], decay, scale, tables[1], tables[2], mask) + (() if labels is None else (labels,))
     return pl.pallas_call(
-        partial(solve_kernel, n),
-        out_shape=jax.ShapeDtypeStruct((length, columns), jnp.float32),
-        in_specs=[vmem] * 7,
+        partial(solve_kernel, n, labels is not None),
+        out_shape=jax.ShapeDtypeStruct(real_field.shape, jnp.float32),
+        in_specs=[vmem] * len(args),
         out_specs=vmem,
         scratch_shapes=[
+            pltpu.VMEM((length // lanes, xs * span, lanes), jnp.float32),
             pltpu.VMEM((span, layers, length), jnp.float32),
+            pltpu.VMEM((2, wide, chunks, xs, lanes), jnp.float32),
+            pltpu.VMEM((2, wide, chunks, xs, lanes), jnp.float32),
             pltpu.VMEM((rows, length), jnp.float32),
             pltpu.VMEM((n - 1, rows, length), jnp.float32),
             pltpu.SemaphoreType.DMA((n - 1,)),
             pltpu.SemaphoreType.DMA((n - 1,)),
+            pltpu.SemaphoreType.DMA((2, parts, wide)),
+            pltpu.SemaphoreType.DMA((2, parts, wide)),
         ],
         compiler_params=pltpu.CompilerParams(
-            collective_id=0, has_side_effects=True, vmem_limit_bytes=40 * 1024 * 1024
+            collective_id=0 if labels is None else 1, has_side_effects=True, vmem_limit_bytes=40 * 1024 * 1024
         ),
         cost_estimate=pl.CostEstimate(
-            flops=4 * length * length * columns, bytes_accessed=8 * length * columns, transcendentals=0
+            flops=8 * xs * span * length * length, bytes_accessed=8 * xs * span * length, transcendentals=0
         ),
-        name="lines",
-    )(field, tables[0], decay, scale, tables[1], tables[2], mask)
-
-
-def solve(real_field, tables, decay, scale, mask):
-    table = tables[0]
-    span_wide, span_narrow, length = real_field.shape
-    wide = lax.axis_size("wide")
-    layers = length // wide
-    waves = jnp.einsum("xyz,zk->xyk", real_field, table, precision=highest)
-    blocks = waves.reshape(span_wide, span_narrow, wide, layers).transpose(2, 0, 1, 3)
-    arrived = lax.all_to_all(
-        blocks.reshape(wide, span_wide, span_narrow * layers), "wide", split_axis=0, concat_axis=0, tiled=True
-    )
-    lines = solve_lines(arrived.reshape(length, span_narrow * layers), tables, decay, scale, mask, layers)
-    returned = lax.all_to_all(
-        lines.reshape(wide, span_wide, span_narrow * layers), "wide", split_axis=0, concat_axis=0, tiled=True
-    )
-    waves = returned.reshape(wide, span_wide, span_narrow, layers).transpose(1, 2, 0, 3)
-    return jnp.einsum("xyk,kz->xyz", waves.reshape(span_wide, span_narrow, length), table, precision=highest)
+        name="solve" if labels is None else "solve_signed",
+    )(*args)
 
 
 def extended(x, sides, width):
@@ -256,15 +363,13 @@
     corner = (jnp.arange(length, dtype=jnp.int32)[None, :] == 0) & (place == 0)
     norm = float(length) ** 2
     heat_field = solve(
-        sources.astype(jnp.float32), tables, heat_decay, heat_decay * (1.0 / (heat_time * norm)),
+        sources, tables, heat_decay, heat_decay * (1.0 / (heat_time * norm)),
         jnp.zeros((1, length), jnp.float32),
     )
     divergence = flow_divergence(heat_field, grad_floor)
-    potential = solve(
-        divergence, tables, line_decay, line_decay * (-1.0 / norm), jnp.where(corner, -1.0 / norm, 0.0)
+    return solve(
+        divergence, tables, line_decay, line_decay * (-1.0 / norm), jnp.where(corner, -1.0 / norm, 0.0), labels
     )
-    signs = (2 * labels - 1).astype(jnp.float32)
-    return signs * potential
 
 
 def solution(mesh):

time: 268 us -> 171 us (0.64)
  Pallas kernels: 37.7 us -> 140 us
  blocking collectives: 60.1 us -> 0 us
  waiting for transfers between devices: 58.6 us -> 6.37 us
  local copies, waits for them, and re-layouts: 57.7 us -> 8.04 us
  matrix products: 29.4 us -> 0 us
  starting transfers between devices: 15.5 us -> 6.57 us
    pallas_call x2, Pallas kernels: 37.7 us -> 140 us  [solve(): pl.pallas_call(partial(solve_kernel, n, labels is not None), out_shape=ja...]
    all_to_all x2 -> x0, blocking collectives: 60.1 us -> none  [solve(): lax.all_to_all(lines.reshape(wide, span_wide, span_narrow * layers), 'wid...]
    all_to_all x2 -> x0, waiting for transfers between devices: 51.7 us -> none  [solve(): lax.all_to_all(blocks.reshape(wide, span_wide, span_narrow * layers), 'wi...]
    dot_general x4 -> x0, matrix products: 29.4 us -> none  [the longest x2 19.2 us: solve(): jnp.einsum('xyk,kz->xyz', waves.reshape(span_wide, span_narrow, length),...]
    transpose x4 -> x0, local copies, waits for them, and re-layouts: 27.8 us -> none  [the longest x2 13.9 us: solve(): waves.reshape(span_wide, span_narrow, wide, layers).transpose(2, 0, 1, 3)]
    reshape x4 -> x0, local copies, waits for them, and re-layouts: 24.5 us -> none  [the longest x2 15 us: solve(): blocks.reshape(wide, span_wide, span_narrow * layers)]
    all_to_all x2 -> x0, starting transfers between devices: 8.92 us -> none  [solve(): lax.all_to_all(blocks.reshape(wide, span_wide, span_narrow * layers), 'wi...]
    unnamed x10 -> x17, local copies, waits for them, and re-layouts: 0.02 us -> 5.49 us
  transfers between devices with their start and end apart: 6 -> 4, of which waited for: 5 -> 3; matrix products, arithmetic and copies ran while one was open for 1% -> 0% of each run, Pallas kernels for 0% -> 0%
where the time goes in v3:
time: 171 us
  Pallas kernels  140 us (82%)
  other arithmetic  9.8 us (6%)
  local copies, waits for them, and re-layouts  8.04 us (5%)
  starting transfers between devices  6.57 us (4%)
  waiting for transfers between devices  6.37 us (4%)
    pallas_call x2, Pallas kernels, solve(): pl.pallas_call(partial(solve_kernel, n, labels is not None), out_shape=ja...  140 us
    ppermute x2, waiting for transfers between devices, extended(): before = lax.ppermute(last, axis, up)  5.54 us
    unnamed x17, local copies, waits for them, and re-layouts  5.49 us
    mul x1, other arithmetic, flow_divergence(): flow_z = (grad_z * inverse)[1:-1, 1:-1]  4.76 us
    ppermute x2, starting transfers between devices, extended(): after = lax.ppermute(initial, axis, down)  3.82 us
  transfers between devices with their start and end apart: 4, of which 3 were waited for; matrix products, arithmetic and copies ran while one was open for 0% of the time, Pallas kernels for 0%

profile of v3, /device:TPU:0, one launch (start us, length us, event | category | flops | bytes accessed | tf_op | source)
XLA Modules:
  0.0 170.6 jit_solution(18157761839666640527)
XLA Ops:
  0.0 0.8 broadcast_multiply_fusion.1
  0.8 1.6 copy-done.1
  2.4 0.9 copy-done.2
  3.3 0.8 copy-done.4
  4.1 0.7 copy-done.6
  4.8 72.0 %solve.1 = f32[32,64,256]{2,1,0:T(8,128)S(1)} custom-call(s32[32,64,256]{2,1,0:T(8,128)S(1)} %copy-done.1, f32[256,256]{1,0:T(8,128)S(1)} %copy-done.2, f32[32,256]{1,0:T(8,128)S(1)} %get-tuple-element.24.decay, f32[32,256]{1,0:T(8,128)S(1)} %get-tuple-element.23.scale, f32[64,88]{1,0:T(8,128)S(1)} %copy-done.4, f32[8,64]{1,0:T(8,128)S(1)} %copy-done.6, ...), custom_call_target="tpu_custom_call" | custom-call | flops 1073741824 | bytes 4194304 | tf_op jit(solution)/shard_map/solve/pallas_call | solution.py:287
  76.8 0.6 collective-permute-start
  77.4 2.1 %collective-permute-start.1 = (f32[2,64,256]{2,1,0:T(8,128)S(1)}, f32[2,64,256]{2,1,0:T(8,128)S(1)}, u32[]{:S(2)}, u32[]{:S(2)}) collective-permute-start(f32[2,64,256]{2,1,0:T(8,128)S(1)} %get-tuple-element.20), channel_id=1, source_target_pairs={{4,0},{8,4},{12,8},{16,12},{20,16},{24,20},{28,24},{0,28},{5,1},{9... | collective-permute-start | bytes 393224 | tf_op jit(solution)/shard_map/ppermute | solution.py:322
  79.5 0.8 broadcast_multiply_fusion
  80.3 2.5 %collective-permute-done = f32[2,64,256]{2,1,0:T(8,128)S(1)} collective-permute-done((f32[2,64,256]{2,1,0:T(8,128)S(1)}, f32[2,64,256]{2,1,0:T(8,128)S(1)}, u32[]{:S(2)}, u32[]{:S(2)}) %collective-permute-start) | collective-permute-done | bytes 131104 | tf_op jit(solution)/shard_map/ppermute | solution.py:321
  82.8 0.0 collective-permute-done.1
  82.8 0.1 pad_maximum_fusion.9
  82.8 2.2 %collective-permute-start.2 = (f32[36,2,256]{2,1,0:T(2,128)S(1)}, f32[36,2,256]{2,1,0:T(2,128)S(1)}, u32[]{:S(2)}, u32[]{:S(2)}) collective-permute-start(f32[36,2,256]{2,1,0:T(2,128)S(1)} %get-tuple-element.17), channel_id=1, source_target_pairs={{0,1},{1,2},{2,3},{3,0},{4,5},{5,6},{6,7},{7,4},{8,9},{9,10},{10,1... | collective-permute-start | bytes 221192 | tf_op jit(solution)/shard_map/ppermute | solution.py:321
  85.0 1.7 collective-permute-start.3
  86.7 3.0 %collective-permute-done.2 = f32[36,2,256]{2,1,0:T(2,128)S(1)} collective-permute-done((f32[36,2,256]{2,1,0:T(2,128)S(1)}, f32[36,2,256]{2,1,0:T(2,128)S(1)}, u32[]{:S(2)}, u32[]{:S(2)}) %collective-permute-start.2) | collective-permute-done | bytes 73760 | tf_op jit(solution)/shard_map/ppermute | solution.py:321
  89.8 0.8 collective-permute-done.3
  90.6 0.3 pad_maximum_fusion
  90.9 0.9 fusion.10
  91.8 0.4 fusion.11
  92.2 4.8 %fusion.9 = (f32[34,66,256]{2,1,0:T(8,128)S(1)}, f32[34,66,256]{2,1,0:T(8,128)S(1)}) fusion(f32[34,66,255]{2,1,0:T(8,128)S(1)} %get-tuple-element.8, f32[34,66,1]{2,1,0:T(8,128)S(1)} %get-tuple-element.10, f32[34,66,1]{2,1,0:T(8,128)S(1)} %get-tuple-element.9, f32[34,66,255]{2,1,0:T(8,128)S(1)} %get-tuple-element.7, ...), kind=kLoop, calls=%fused_computation.30 | loop fusion | flops 12638208 | bytes 16293888 | tf_op jit(solution)/shard_map/mul | solution.py:340
  97.0 0.9 fusion.13
  97.8 0.4 fusion.12
  98.3 1.7 %fusion.7 = (f32[34,66,256]{2,1,0:T(8,128)S(1)}, f32[34,66,256]{2,1,0:T(8,128)S(1)}) fusion(f32[34,66,256]{2,1,0:T(8,128)S(1)} %get-tuple-element.6, f32[36,68,256]{2,1,0:T(8,128)S(1)} %pad_maximum_fusion, f32[2,64,256]{2,1,0:T(8,128)S(1)} %collective-permute-done.1, f32[32,64,256]{2,1,0:T(8,128)S(1)} %solve.1, f32[2,64,256]{2,1,0:T(8,128)S(1)} %collective-permute-done, ...), kind=kLoop, calls=%fused_computation.20 | loop fusion | flops 6893568 | bytes 13996032 | tf_op jit(solution)/shard_map/mul | solution.py:338
  100.0 0.0 copy-start
  100.0 0.0 copy-start.3
  100.0 0.0 copy-start.5
  100.0 0.0 copy-start.7
  100.1 1.4 fusion.6.field
  101.4 0.2 copy-done
  101.6 0.0 copy-done.3
  101.6 67.7 %solve_signed.1 = f32[32,64,256]{2,1,0:T(8,128)S(1)} custom-call(f32[32,64,256]{2,1,0:T(8,128)S(1)} %fusion.6.field, f32[256,256]{1,0:T(8,128)S(1)} %copy-done.3, f32[32,256]{1,0:T(8,128)S(1)} %get-tuple-element.22.decay, f32[32,256]{1,0:T(8,128)S(1)} %get-tuple-element.21.scale, f32[64,88]{1,0:T(8,128)S(1)} %copy-done.5, f32[8,64]{1,0:T(8,128)S(1)} %copy-done.7, ...), custom_call_target="tpu_custom_call" | custom-call | flops 1073741824 | bytes 4194304 | tf_op jit(solution)/shard_map/solve_signed/pallas_call | solution.py:287
  169.3 1.3 copy.9
  (9 shorter events, 0.0 us)
Async XLA Ops:
  0.8 1.6 copy-start.1
  2.4 0.9 copy-start.2
  3.3 0.8 copy-start.4
  4.1 0.7 copy-start.6
  76.8 6.0 %collective-permute-start = (f32[2,64,256]{2,1,0:T(8,128)S(1)}, f32[2,64,256]{2,1,0:T(8,128)S(1)}, u32[]{:S(2)}, u32[]{:S(2)}) collective-permute-start(f32[2,64,256]{2,1,0:T(8,128)S(1)} %get-tuple-element.19), channel_id=1, source_target_pairs={{0,4},{4,8},{8,12},{12,16},{16,20},{20,24},{24,28},{28,0},{1,5},{5... | collective-permute-start | bytes 393224 | tf_op jit(solution)/shard_map/ppermute | solution.py:321
  77.4 5.4 %collective-permute-start.1 = (f32[2,64,256]{2,1,0:T(8,128)S(1)}, f32[2,64,256]{2,1,0:T(8,128)S(1)}, u32[]{:S(2)}, u32[]{:S(2)}) collective-permute-start(f32[2,64,256]{2,1,0:T(8,128)S(1)} %get-tuple-element.20), channel_id=1, source_target_pairs={{4,0},{8,4},{12,8},{16,12},{20,16},{24,20},{28,24},{0,28},{5,1},{9... | collective-permute-start | bytes 393224 | tf_op jit(solution)/shard_map/ppermute | solution.py:322
  82.8 6.9 %collective-permute-start.2 = (f32[36,2,256]{2,1,0:T(2,128)S(1)}, f32[36,2,256]{2,1,0:T(2,128)S(1)}, u32[]{:S(2)}, u32[]{:S(2)}) collective-permute-start(f32[36,2,256]{2,1,0:T(2,128)S(1)} %get-tuple-element.17), channel_id=1, source_target_pairs={{0,1},{1,2},{2,3},{3,0},{4,5},{5,6},{6,7},{7,4},{8,9},{9,10},{10,1... | collective-permute-start | bytes 221192 | tf_op jit(solution)/shard_map/ppermute | solution.py:321
  85.0 5.6 %collective-permute-start.3 = (f32[36,2,256]{2,1,0:T(2,128)S(1)}, f32[36,2,256]{2,1,0:T(2,128)S(1)}, u32[]{:S(2)}, u32[]{:S(2)}) collective-permute-start(f32[36,2,256]{2,1,0:T(2,128)S(1)} %get-tuple-element.18), channel_id=1, source_target_pairs={{1,0},{2,1},{3,2},{0,3},{5,4},{6,5},{7,6},{4,7},{9,8},{10,9},{11,1... | collective-permute-start | bytes 221192 | tf_op jit(solution)/shard_map/ppermute | solution.py:322
  100.0 1.6 copy-start
  100.0 1.6 copy-start.3
  100.0 1.6 copy-start.5
  100.0 1.6 copy-start.7

commit v4 on v3

--- a/solution.py
+++ b/solution.py
@@ -12,6 +12,7 @@
 highest = lax.Precision.HIGHEST
 moment_rows = 8
 lanes = 128
+margin = 8
 
 
 def cas_table(length):
@@ -55,9 +56,69 @@
     return result
 
 
-def solve_kernel(n, signed, field, table, decay, scale, green, moments, mask, *rest):
+def flow_stage(n, grad_floor, field, partial_sum, flow_x, padded, leaving, landing, send_sem, recv_sem):
+    xs, span, length = field.shape
+    me = lax.axis_index("narrow")
+    here = lax.axis_index("wide")
+    wide = lax.axis_size("wide")
+    inside = pl.ds(margin, span)
+
+    def transfer(k, src, dst, target):
+        copy = pltpu.make_async_remote_copy(
+            src_ref=src, dst_ref=dst, send_sem=send_sem.at[k], recv_sem=recv_sem.at[k],
+            device_id=target, device_id_type=pl.DeviceIdType.MESH,
+        )
+        copy.start()
+        return copy
+
+    first = transfer(0, field.at[pl.ds(xs - 2, 2)], padded.at[pl.ds(0, 2), inside], {"wide": lax.rem(here + 1, wide)})
+    second = transfer(1, field.at[pl.ds(0, 2)], padded.at[pl.ds(xs + 2, 2), inside], {"wide": lax.rem(here + wide - 1, wide)})
+    edge = jnp.zeros((xs + 4, margin, length), jnp.float32)
+    padded[:, 0:margin, :] = edge
+    padded[:, margin + span :, :] = edge
+
+    def fill(x, carry):
+        padded[x + 2, margin : margin + span, :] = field[x]
+        return carry
+
+    lax.fori_loop(0, xs, fill, 0)
+    first.wait()
+    second.wait()
+    for row in range(2):
+        leaving[0, row] = padded[:, margin + span - 2 + row, :]
+        leaving[1, row] = padded[:, margin + row, :]
+    third = transfer(2, leaving.at[0], landing.at[0], {"narrow": lax.rem(me + 1, n)})
+    fourth = transfer(3, leaving.at[1], landing.at[1], {"narrow": lax.rem(me + n - 1, n)})
+    third.wait()
+    fourth.wait()
+    for row in range(2):
+        padded[:, margin - 2 + row, :] = landing[0, row]
+        padded[:, margin + span + row, :] = landing[1, row]
+
+    def central(values, dim):
+        size = values.shape[dim]
+        return 0.5 * (pltpu.roll(values, size - 1, dim) - pltpu.roll(values, 1, dim))
+
+    def plane(p, carry):
+        values = padded[p]
+        grad_x = 0.5 * (padded[p + 1] - padded[p - 1])
+        grad_y = central(values, 0)
+        grad_z = central(values, 1)
+        magnitude = jnp.sqrt(grad_x * grad_x + grad_y * grad_y + grad_z * grad_z)
+        inverse = -1.0 / jnp.maximum(magnitude, grad_floor)
+        flow_x[p - 1] = (grad_x * inverse)[margin : margin + span]
+        total = central(grad_y * inverse, 0) + central(grad_z * inverse, 1)
+        partial_sum[p - 1] = total[margin : margin + span]
+        return carry
+
+    lax.fori_loop(1, xs + 3, plane, 0)
+
+
+def solve_kernel(n, grad_floor, field, table, decay, scale, green, moments, mask, *rest):
+    signed = grad_floor is not None
     labels = rest[0] if signed else None
-    out, waves, work, outgoing, incoming, sent, arrived, send_sem, recv_sem, wide_send, wide_recv = rest[1:] if signed else rest
+    rest = rest[1:] if signed else rest
+    out, waves, work, outgoing, incoming, sent, arrived, send_sem, recv_sem, wide_send, wide_recv = rest[:11]
     xs, span, length = field.shape
     wide = incoming.shape[1]
     layers = length // wide
@@ -81,6 +142,11 @@
 
     lax.fori_loop(1, wide, greet, 0)
 
+    if signed:
+        pl.semaphore_wait(barrier, n - 1 + wide - 1)
+        partial_sum, flow_x = rest[11:13]
+        flow_stage(n, grad_floor, field, *rest[11:])
+
     def block_copy(turn, part, step):
         target = lax.rem(here + step, wide)
         some = pl.ds(part * each, each)
@@ -117,7 +183,13 @@
         lax.fori_loop(1, wide, one, 0)
 
     def transform(c, carry):
-        rows = field[pl.ds(c * step_rows, step_rows)].astype(jnp.float32).reshape(step_rows * span, length)
+        if signed:
+            planes = partial_sum[pl.ds(1 + c * step_rows, step_rows)] + 0.5 * (
+                flow_x[pl.ds(2 + c * step_rows, step_rows)] - flow_x[pl.ds(c * step_rows, step_rows)]
+            )
+        else:
+            planes = field[pl.ds(c * step_rows, step_rows)].astype(jnp.float32)
+        rows = planes.reshape(step_rows * span, length)
         result = jnp.dot(rows, table[...], precision=highest, preferred_element_type=jnp.float32)
         start = pl.multiple_of(c * step_rows * span, step_rows * span)
         for h in range(halves):
@@ -141,7 +213,7 @@
 
     for part in range(parts):
         lax.fori_loop(part * each, (part + 1) * each, split, 0)
-        if part == 0:
+        if part == 0 and not signed:
             pl.semaphore_wait(barrier, n - 1 + wide - 1)
         send_part(0, part)
 
@@ -274,7 +346,7 @@
         finish_part(1, part)
 
 
-def solve(real_field, tables, decay, scale, mask, labels=None):
+def solve(real_field, tables, decay, scale, mask, labels=None, grad_floor=None):
     xs, span, length = real_field.shape
     n = lax.axis_size("narrow")
     wide = lax.axis_size("wide")
@@ -284,8 +356,17 @@
     rows = 2 * layers + moment_rows
     vmem = pl.BlockSpec(memory_space=pltpu.VMEM)
     args = (real_field, tables[0], decay, scale, tables[1], tables[2], mask) + (() if labels is None else (labels,))
+    flow_scratch = [] if labels is None else [
+        pltpu.VMEM((xs + 2, span, length), jnp.float32),
+        pltpu.VMEM((xs + 2, span, length), jnp.float32),
+        pltpu.VMEM((xs + 4, span + 2 * margin, length), jnp.float32),
+        pltpu.VMEM((2, 2, xs + 4, length), jnp.float32),
+        pltpu.VMEM((2, 2, xs + 4, length), jnp.float32),
+        pltpu.SemaphoreType.DMA((4,)),
+        pltpu.SemaphoreType.DMA((4,)),
+    ]
     return pl.pallas_call(
-        partial(solve_kernel, n, labels is not None),
+        partial(solve_kernel, n, grad_floor),
         out_shape=jax.ShapeDtypeStruct(real_field.shape, jnp.float32),
         in_specs=[vmem] * len(args),
         out_specs=vmem,
@@ -300,7 +381,8 @@
             pltpu.SemaphoreType.DMA((n - 1,)),
             pltpu.SemaphoreType.DMA((2, parts, wide)),
             pltpu.SemaphoreType.DMA((2, parts, wide)),
-        ],
+        ]
+        + flow_scratch,
         compiler_params=pltpu.CompilerParams(
             collective_id=0 if labels is None else 1, has_side_effects=True, vmem_limit_bytes=40 * 1024 * 1024
         ),
@@ -309,40 +391,6 @@
         ),
         name="solve" if labels is None else "solve_signed",
     )(*args)
-
-
-def extended(x, sides, width):
-    for axis, dim in sides:
-        peers, length = (lax.axis_size(axis), x.shape[dim])
-        up = [(i, (i + 1) % peers) for i in range(peers)]
-        down = [(j, i) for i, j in up]
-        last = lax.slice_in_dim(x, length - width, length, axis=dim)
-        initial = lax.slice_in_dim(x, 0, width, axis=dim)
-        before = lax.ppermute(last, axis, up)
-        after = lax.ppermute(initial, axis, down)
-        x = jnp.concatenate([before, x, after], axis=dim)
-    return x
-
-
-def central_last(values):
-    return 0.5 * (jnp.roll(values, -1, values.ndim - 1) - jnp.roll(values, 1, values.ndim - 1))
-
-
-def flow_divergence(heat_field, grad_floor):
-    padded = extended(heat_field, (("wide", 0), ("narrow", 1)), 2)
-    grad_x = 0.5 * (padded[2:, 1:-1] - padded[:-2, 1:-1])
-    grad_y = 0.5 * (padded[1:-1, 2:] - padded[1:-1, :-2])
-    grad_z = central_last(padded[1:-1, 1:-1])
-    magnitude = jnp.sqrt(grad_x * grad_x + grad_y * grad_y + grad_z * grad_z)
-    inverse = -1.0 / jnp.maximum(magnitude, grad_floor)
-    flow_x = grad_x * inverse
-    flow_y = grad_y * inverse
-    flow_z = (grad_z * inverse)[1:-1, 1:-1]
-    return (
-        0.5 * (flow_x[2:, 1:-1] - flow_x[:-2, 1:-1])
-        + 0.5 * (flow_y[1:-1, 2:] - flow_y[1:-1, :-2])
-        + central_last(flow_z)
-    )
 
 
 def per_device(sources, labels):
@@ -366,9 +414,9 @@
         sources, tables, heat_decay, heat_decay * (1.0 / (heat_time * norm)),
         jnp.zeros((1, length), jnp.float32),
     )
-    divergence = flow_divergence(heat_field, grad_floor)
     return solve(
-        divergence, tables, line_decay, line_decay * (-1.0 / norm), jnp.where(corner, -1.0 / norm, 0.0), labels
+        heat_field, tables, line_decay, line_decay * (-1.0 / norm), jnp.where(corner, -1.0 / norm, 0.0), labels,
+        grad_floor,
     )
 
 

time: 171 us -> 168 us (0.982)
  Pallas kernels: 140 us -> 160 us
  other arithmetic: 9.8 us -> 0.79 us
  starting transfers between devices: 6.57 us -> 0 us
  waiting for transfers between devices: 6.37 us -> 0 us
  local copies, waits for them, and re-layouts: 8.04 us -> 5.31 us
    pallas_call x2, Pallas kernels: 140 us -> 160 us  [solve(): pl.pallas_call(partial(solve_kernel, n, grad_floor), out_shape=jax.ShapeD...]
    mul x3 -> x0, other arithmetic: 7.27 us -> none  [the longest x1 4.76 us: flow_divergence(): flow_z = (grad_z * inverse)[1:-1, 1:-1]]
    ppermute x4 -> x0, starting transfers between devices: 6.57 us -> none  [the longest x2 3.82 us: extended(): after = lax.ppermute(initial, axis, down)]
    ppermute x4 -> x0, waiting for transfers between devices: 6.37 us -> none  [the longest x2 5.54 us: extended(): before = lax.ppermute(last, axis, up)]
    slice x5 -> x0, local copies, waits for them, and re-layouts: 2.55 us -> none  [the longest x2 1.27 us: central_last(): jnp.roll(values, -1, values.ndim - 1) - jnp.roll(values, 1, values.ndim - 1)]
    unnamed x17 -> x15, local copies, waits for them, and re-layouts: 5.49 us -> 5.31 us
  transfers between devices with their start and end apart: 4 -> 0, of which waited for: 3 -> 0; matrix products, arithmetic and copies ran while one was open for 0% -> 0% of each run, Pallas kernels for 0% -> 0%
where the time goes in v4:
time: 168 us; the launch traced here: 167 us
  Pallas kernels  160 us (95%)
  local copies, waits for them, and re-layouts  5.31 us (3%)
    pallas_call x2, Pallas kernels, solve(): pl.pallas_call(partial(solve_kernel, n, grad_floor), out_shape=jax.ShapeD...  160 us
    unnamed x15, local copies, waits for them, and re-layouts  5.31 us

profile of v4, /device:TPU:0, one launch (start us, length us, event | category | flops | bytes accessed | tf_op | source)
XLA Modules:
  0.0 166.6 jit_solution(10845508713311722718)
XLA Ops:
  0.0 0.8 broadcast_multiply_fusion
  0.8 0.0 copy-start.1
  0.8 1.6 copy-done.1
  2.4 0.0 copy-start.2
  2.4 0.9 copy-done.2
  3.4 0.0 copy-start.4
  3.4 0.8 copy-done.4
  4.1 0.0 copy-start.6
  4.1 0.7 copy-done.6
  4.8 0.0 copy-start
  4.8 0.0 copy-start.3
  4.8 0.0 copy-start.5
  4.8 72.1 %solve.1.field = f32[32,64,256]{2,1,0:T(8,128)S(1)} custom-call(s32[32,64,256]{2,1,0:T(8,128)S(1)} %copy-done.1, f32[256,256]{1,0:T(8,128)S(1)} %copy-done.2, f32[32,256]{1,0:T(8,128)S(1)} %get-tuple-element.9.decay, f32[32,256]{1,0:T(8,128)S(1)} %get-tuple-element.10.scale, f32[64,88]{1,0:T(8,128)S(1)} %copy-done.4, f32[8,64]{1,0:T(8,128)S(1)} %copy-done.6, ...), custom_call_target="tpu_custom_call" | custom-call | flops 1073741824 | bytes 4194304 | tf_op jit(solution)/shard_map/solve/pallas_call | solution.py:368
  76.9 0.0 copy-done
  76.9 0.0 copy-done.3
  76.9 0.0 copy-done.5
  76.9 88.3 %solve_signed.1 = f32[32,64,256]{2,1,0:T(8,128)S(1)} custom-call(f32[32,64,256]{2,1,0:T(8,128)S(1)} %solve.1.field, f32[256,256]{1,0:T(8,128)S(1)} %copy-done.3, f32[32,256]{1,0:T(8,128)S(1)} %get-tuple-element.6.decay, f32[32,256]{1,0:T(8,128)S(1)} %get-tuple-element.5.scale, f32[64,88]{1,0:T(8,128)S(1)} %copy-done.5, f32[8,64]{1,0:T(8,128)S(1)} %copy-done.6, ...), custom_call_target="tpu_custom_call" | custom-call | flops 1073741824 | bytes 4194304 | tf_op jit(solution)/shard_map/solve_signed/pallas_call | solution.py:368
  165.3 1.3 copy.9
  (2 shorter events, 0.0 us)
Async XLA Ops:
  0.8 1.6 copy-start.1
  2.4 0.9 copy-start.2
  3.4 0.8 copy-start.4
  4.1 0.7 copy-start.6
  4.8 72.1 %copy-start = (s32[32,64,256]{2,1,0:T(8,128)S(1)}, s32[32,64,256]{2,1,0:T(8,128)}, u32[]{:S(2)}) copy-start(s32[32,64,256]{2,1,0:T(8,128)} %rest_0_.1) | copy-start | bytes 6291460
  4.8 72.1 %copy-start.3 = (f32[256,256]{1,0:T(8,128)S(1)}, f32[256,256]{1,0:T(8,128)}, u32[]{:S(2)}) copy-start(f32[256,256]{1,0:T(8,128)} %constant.12.clone.table) | copy-start | bytes 786436
  4.8 72.1 %copy-start.5 = (f32[64,88]{1,0:T(8,128)S(1)}, f32[64,88]{1,0:T(8,128)}, u32[]{:S(2)}) copy-start(f32[64,88]{1,0:T(8,128)} %constant.32.clone.green) | copy-start | bytes 67588

commit v5 on v4

--- a/solution.py
+++ b/solution.py
@@ -228,19 +228,20 @@
         work[pl.ds(c * group, group)] = block.reshape(group, layers, length)
         return carry
 
-    for part in range(parts):
-        receive_part(0, part)
-        lax.fori_loop(part * each, (part + 1) * each, to_waves, 0)
-
-    column = work[:, 0, :]
-    sent[2 * layers :, :] = jnp.dot(moments[...], column, precision=highest, preferred_element_type=jnp.float32)
-
     def ahead(j, v):
         v = work[j] + r * v
         work[j] = v
         return v
 
-    v_last = lax.fori_loop(0, span, ahead, jnp.zeros_like(r), unroll=4)
+    v_last = jnp.zeros_like(r)
+    columns = []
+    for part in range(parts):
+        receive_part(0, part)
+        lax.fori_loop(part * each, (part + 1) * each, to_waves, 0)
+        columns.append(work[part * rows_each : (part + 1) * rows_each, 0, :])
+        v_last = lax.fori_loop(part * rows_each, (part + 1) * rows_each, ahead, v_last, unroll=4)
+    column = jnp.concatenate(columns, axis=0)
+    sent[2 * layers :, :] = jnp.dot(moments[...], column, precision=highest, preferred_element_type=jnp.float32)
 
     def back(i, u):
         j = span - 1 - i
@@ -352,7 +353,7 @@
     wide = lax.axis_size("wide")
     layers = length // wide
     chunks = span * layers // lanes
-    parts = min(4, chunks)
+    parts = min(8, chunks)
     rows = 2 * layers + moment_rows
     vmem = pl.BlockSpec(memory_space=pltpu.VMEM)
     args = (real_field, tables[0], decay, scale, tables[1], tables[2], mask) + (() if labels is None else (labels,))

time: 168 us -> 166 us (0.988)
  no operation moved by 1% of the time
where the time goes in v5:
time: 166 us
  Pallas kernels  160 us (96%)
  local copies, waits for them, and re-layouts  5.31 us (3%)
    pallas_call x2, Pallas kernels, solve(): pl.pallas_call(partial(solve_kernel, n, grad_floor), out_shape=jax.ShapeD...  160 us
    unnamed x15, local copies, waits for them, and re-layouts  5.31 us

profile of v5, /device:TPU:0, one launch (start us, length us, event | category | flops | bytes accessed | tf_op | source)
XLA Modules:
  0.0 166.1 jit_solution(14313882286476882447)
XLA Ops:
  0.0 0.8 broadcast_multiply_fusion
  0.8 0.0 copy-start.1
  0.8 1.6 copy-done.1
  2.4 0.0 copy-start.2
  2.4 0.9 copy-done.2
  3.4 0.0 copy-start.4
  3.4 0.8 copy-done.4
  4.1 0.0 copy-start.6
  4.1 0.7 copy-done.6
  4.8 0.0 copy-start
  4.8 0.0 copy-start.3
  4.8 0.0 copy-start.5
  4.8 70.5 %solve.1.field = f32[32,64,256]{2,1,0:T(8,128)S(1)} custom-call(s32[32,64,256]{2,1,0:T(8,128)S(1)} %copy-done.1, f32[256,256]{1,0:T(8,128)S(1)} %copy-done.2, f32[32,256]{1,0:T(8,128)S(1)} %get-tuple-element.9.decay, f32[32,256]{1,0:T(8,128)S(1)} %get-tuple-element.10.scale, f32[64,88]{1,0:T(8,128)S(1)} %copy-done.4, f32[8,64]{1,0:T(8,128)S(1)} %copy-done.6, ...), custom_call_target="tpu_custom_call" | custom-call | flops 1073741824 | bytes 4194304 | tf_op jit(solution)/shard_map/solve/pallas_call | solution.py:369
  75.4 0.0 copy-done
  75.4 0.0 copy-done.3
  75.4 0.0 copy-done.5
  75.4 89.3 %solve_signed.1 = f32[32,64,256]{2,1,0:T(8,128)S(1)} custom-call(f32[32,64,256]{2,1,0:T(8,128)S(1)} %solve.1.field, f32[256,256]{1,0:T(8,128)S(1)} %copy-done.3, f32[32,256]{1,0:T(8,128)S(1)} %get-tuple-element.6.decay, f32[32,256]{1,0:T(8,128)S(1)} %get-tuple-element.5.scale, f32[64,88]{1,0:T(8,128)S(1)} %copy-done.5, f32[8,64]{1,0:T(8,128)S(1)} %copy-done.6, ...), custom_call_target="tpu_custom_call" | custom-call | flops 1073741824 | bytes 4194304 | tf_op jit(solution)/shard_map/solve_signed/pallas_call | solution.py:369
  164.7 1.3 copy.9
  (2 shorter events, 0.0 us)
Async XLA Ops:
  0.8 1.6 copy-start.1
  2.4 0.9 copy-start.2
  3.4 0.8 copy-start.4
  4.1 0.7 copy-start.6
  4.8 70.6 %copy-start = (s32[32,64,256]{2,1,0:T(8,128)S(1)}, s32[32,64,256]{2,1,0:T(8,128)}, u32[]{:S(2)}) copy-start(s32[32,64,256]{2,1,0:T(8,128)} %rest_0_.1) | copy-start | bytes 6291460
  4.8 70.6 %copy-start.3 = (f32[256,256]{1,0:T(8,128)S(1)}, f32[256,256]{1,0:T(8,128)}, u32[]{:S(2)}) copy-start(f32[256,256]{1,0:T(8,128)} %constant.12.clone.table) | copy-start | bytes 786436
  4.8 70.6 %copy-start.5 = (f32[64,88]{1,0:T(8,128)S(1)}, f32[64,88]{1,0:T(8,128)}, u32[]{:S(2)}) copy-start(f32[64,88]{1,0:T(8,128)} %constant.32.clone.green) | copy-start | bytes 67588

commit v6 on v5

--- a/solution.py
+++ b/solution.py
@@ -160,7 +160,8 @@
         )
 
     def send_part(turn, part):
-        def one(step, carry):
+        def one(count, carry):
+            step = 1 + lax.rem(count + wide // 2 - 2, wide - 1)
             block_copy(turn, part, step).start()
             return carry
 

time: 166 us -> 166 us (level)
  no operation moved by 1% of the time
where the time goes in v6:
time: 166 us
  Pallas kernels  160 us (96%)
  local copies, waits for them, and re-layouts  5.31 us (3%)
    pallas_call x2, Pallas kernels, solve(): pl.pallas_call(partial(solve_kernel, n, grad_floor), out_shape=jax.ShapeD...  160 us
    unnamed x15, local copies, waits for them, and re-layouts  5.31 us

profile of v6, /device:TPU:0, one launch (start us, length us, event | category | flops | bytes accessed | tf_op | source)
XLA Modules:
  0.0 166.1 jit_solution(14586702005069950451)
XLA Ops:
  0.0 0.8 broadcast_multiply_fusion
  0.8 0.0 copy-start.1
  0.8 1.6 copy-done.1
  2.4 0.0 copy-start.2
  2.4 0.9 copy-done.2
  3.4 0.0 copy-start.4
  3.4 0.8 copy-done.4
  4.1 0.0 copy-start.6
  4.1 0.7 copy-done.6
  4.8 0.0 copy-start
  4.8 0.0 copy-start.3
  4.8 0.0 copy-start.5
  4.8 69.7 %solve.1.field = f32[32,64,256]{2,1,0:T(8,128)S(1)} custom-call(s32[32,64,256]{2,1,0:T(8,128)S(1)} %copy-done.1, f32[256,256]{1,0:T(8,128)S(1)} %copy-done.2, f32[32,256]{1,0:T(8,128)S(1)} %get-tuple-element.9.decay, f32[32,256]{1,0:T(8,128)S(1)} %get-tuple-element.10.scale, f32[64,88]{1,0:T(8,128)S(1)} %copy-done.4, f32[8,64]{1,0:T(8,128)S(1)} %copy-done.6, ...), custom_call_target="tpu_custom_call" | custom-call | flops 1073741824 | bytes 4194304 | tf_op jit(solution)/shard_map/solve/pallas_call | solution.py:370
  74.5 0.0 copy-done
  74.5 0.0 copy-done.3
  74.5 0.0 copy-done.5
  74.6 90.2 %solve_signed.1 = f32[32,64,256]{2,1,0:T(8,128)S(1)} custom-call(f32[32,64,256]{2,1,0:T(8,128)S(1)} %solve.1.field, f32[256,256]{1,0:T(8,128)S(1)} %copy-done.3, f32[32,256]{1,0:T(8,128)S(1)} %get-tuple-element.6.decay, f32[32,256]{1,0:T(8,128)S(1)} %get-tuple-element.5.scale, f32[64,88]{1,0:T(8,128)S(1)} %copy-done.5, f32[8,64]{1,0:T(8,128)S(1)} %copy-done.6, ...), custom_call_target="tpu_custom_call" | custom-call | flops 1073741824 | bytes 4194304 | tf_op jit(solution)/shard_map/solve_signed/pallas_call | solution.py:370
  164.7 1.3 copy.9
  (2 shorter events, 0.0 us)
Async XLA Ops:
  0.8 1.6 copy-start.1
  2.4 0.9 copy-start.2
  3.4 0.8 copy-start.4
  4.1 0.7 copy-start.6
  4.8 69.7 %copy-start = (s32[32,64,256]{2,1,0:T(8,128)S(1)}, s32[32,64,256]{2,1,0:T(8,128)}, u32[]{:S(2)}) copy-start(s32[32,64,256]{2,1,0:T(8,128)} %rest_0_.1) | copy-start | bytes 6291460
  4.8 69.7 %copy-start.3 = (f32[256,256]{1,0:T(8,128)S(1)}, f32[256,256]{1,0:T(8,128)}, u32[]{:S(2)}) copy-start(f32[256,256]{1,0:T(8,128)} %constant.12.clone.table) | copy-start | bytes 786436
  4.8 69.7 %copy-start.5 = (f32[64,88]{1,0:T(8,128)S(1)}, f32[64,88]{1,0:T(8,128)}, u32[]{:S(2)}) copy-start(f32[64,88]{1,0:T(8,128)} %constant.32.clone.green) | copy-start | bytes 67588
